TPU v7x, 32 devices: a whole 2x2x4 slice. The times are simulated.
32 devices in a mesh: aux: 4 (over y, x), pair: 8 (over z, core).
Axes of the slice: x: 2, y: 2, z: 4, core: 2. Of those that a mesh axis runs over, the one named last changes fastest.
Arguments:
- orbital_slabs: bfloat16 [32, 1024, 768], P('pair', 'aux'), may hold values from -2.5 to 2.5
- pno_maps: bfloat16 [128, 768, 256], P('pair'), may hold values from -0.21875 to 0.21875
- intersections: bfloat16 [128, 8, 256, 256], P('pair', 'aux'), may hold values from -0.375 to 0.375
- pno_energy: float32 [128, 256], P('pair'), may hold values from 0.25 to 2
- occ_energy: float32 [32], replicated, may hold values from -1 to -0.25
- pair_orbitals: int32 [128, 2], replicated, may hold values from 0 to 31, as said below
- partners: int32 [128, 8], replicated, may hold values from 0 to 127, as said below
- live: int32 [128], P('pair'), may hold values from 0 to 1, as said below
Outputs:
- amplitudes: bfloat16 [128, 256, 256], P('pair')
- pair_energy: float32 [128], P('pair')
Inputs may be any that keep to these rules, and one draw needn't show every extreme that they name: `pair_orbitals`: each pair names two different orbitals. The pairs of one cluster of 16 slots (padding slots too) name at most one orbital of each block of 4 consecutive orbitals. `partners`: every partner is a live pair. All 128 partner entries of one cluster of 16 slots together name at most one pair of each cluster. In each cluster of 16 slots the live pairs come first and there is at least one; some cluster is full.
All inputs are finite; a program needn't handle non-finite values.
Results may differ from a plain program's by a relative error of at most 0.0066.
Values may be sent and summed in bfloat16 or wider, within the bound.
A program may use at most 128 MiB of HBM per device.

v0:
```python
import jax
import jax.numpy as jnp
from jax import lax
from jax.sharding import PartitionSpec as P

ITERS = 2


damping = 0.7


def on_device(
    orbital_slabs, pno_maps, intersections, pno_energy, occ_energy, pair_orbitals, partners, live
):
    clusters = lax.axis_size("pair")
    groups = lax.axis_size("aux")
    cluster = lax.axis_index("pair")
    aux_row = lax.axis_index("aux")
    orb_count = orbital_slabs.shape[0]
    pair_count = pno_maps.shape[0]
    width = intersections.shape[-1]
    wanted = pair_orbitals.reshape(clusters, 2 * pair_count)
    owned = cluster * orb_count + jnp.arange(orb_count, dtype=jnp.int32)
    needed = jnp.any(wanted[:, :, None] == owned[None, None, :], axis=1).astype(jnp.bfloat16)
    outgoing = jnp.dot(
        needed, orbital_slabs.reshape(orb_count, -1), preferred_element_type=jnp.float32
    )
    outgoing = outgoing.astype(jnp.bfloat16).reshape((clusters,) + orbital_slabs.shape[1:])
    my_orbitals = lax.dynamic_slice_in_dim(pair_orbitals, cluster * pair_count, pair_count, 0)
    owner_index = my_orbitals // orb_count
    incoming = lax.all_to_all(outgoing, "pair", split_axis=0, concat_axis=0, tiled=True)
    left = jnp.take(incoming, owner_index[:, 0], axis=0)
    right = jnp.take(incoming, owner_index[:, 1], axis=0)
    left_pno = jnp.einsum(
        "pav,pvn->pan", left, pno_maps, preferred_element_type=jnp.float32
    ).astype(jnp.bfloat16)
    right_pno = jnp.einsum(
        "pav,pvn->pan", right, pno_maps, preferred_element_type=jnp.float32
    ).astype(jnp.bfloat16)
    left_pno, right_pno = (left_pno, right_pno)
    partial_coulomb = jnp.einsum(
        "pan,pam->pnm", left_pno, right_pno, preferred_element_type=jnp.float32
    )
    occupied = jnp.sum(jnp.take(occ_energy, my_orbitals), axis=1)
    denominator = pno_energy[:, :, None] + pno_energy[:, None, :] - occupied[:, None, None]
    weights = live.astype(jnp.float32)
    share = pair_count // groups
    all_refs = partners.reshape(clusters, pair_count, -1)
    coulomb = lax.psum_scatter(partial_coulomb, "aux", scatter_dimension=0, tiled=True)
    denominator = lax.dynamic_slice_in_dim(denominator, aux_row * share, share, 0)
    weights = lax.dynamic_slice_in_dim(weights, aux_row * share, share, 0)
    row_refs = lax.dynamic_slice_in_dim(all_refs, aux_row * share, share, 1).reshape(clusters, -1)
    used_intersections = lax.all_to_all(
        intersections, "aux", split_axis=0, concat_axis=1, tiled=True
    )
    weights = weights[:, None, None]
    amplitude = -weights * coulomb / denominator
    coulomb_half = coulomb.astype(jnp.bfloat16)
    my_pairs = cluster * pair_count + jnp.arange(pair_count, dtype=jnp.int32)
    sending = jnp.any(row_refs[:, :, None] == my_pairs[None, None, :], axis=1).astype(jnp.bfloat16)
    my_refs = lax.dynamic_slice_in_dim(row_refs, cluster, 1, 0).reshape(-1)
    ref_sources = my_refs // pair_count
    ref_rows = used_intersections.shape[0]
    ref_cols = used_intersections.shape[1]
    flat_intersections = used_intersections.reshape(ref_rows * ref_cols, width, width)
    for sweep in range(ITERS):
        local_half = amplitude.astype(jnp.bfloat16)
        cluster_half = lax.all_gather(local_half, "aux", axis=0, tiled=True)
        outgoing_amps = jnp.dot(
            sending, cluster_half.reshape(pair_count, -1), preferred_element_type=jnp.float32
        )
        outgoing_amps = outgoing_amps.astype(jnp.bfloat16).reshape(clusters, width, width)
        fetched = jnp.take(
            lax.all_to_all(outgoing_amps, "pair", split_axis=0, concat_axis=0, tiled=True),
            ref_sources,
            axis=0,
        )
        rotated = jnp.einsum(
            "kab,kbc->kac", flat_intersections, fetched, preferred_element_type=jnp.float32
        )
        rotated = rotated.astype(jnp.bfloat16)
        rotated = rotated.reshape(ref_rows, ref_cols, width, width)
        coupling_terms = jnp.einsum(
            "prac,prdc->pad", rotated, used_intersections, preferred_element_type=jnp.float32
        )
        product = jnp.einsum(
            "pab,pcb->pac", local_half, coulomb_half, preferred_element_type=jnp.float32
        ).astype(jnp.bfloat16)
        quadratic = (
            jnp.einsum("pac,pcd->pad", product, local_half, preferred_element_type=jnp.float32)
            / width
        )
        residual = coulomb + denominator * amplitude - coupling_terms + quadratic
        amplitude = weights * (amplitude - damping * residual / denominator)
    result = amplitude.astype(jnp.bfloat16)
    energy = weights[:, 0, 0] * jnp.sum(coulomb * amplitude, axis=(1, 2))
    result, energy = (
        lax.all_gather(result, "aux", axis=0, tiled=True),
        lax.all_gather(energy.astype(jnp.bfloat16), "aux", axis=0, tiled=True).astype(energy.dtype),
    )
    return (result, energy)


def solution(mesh):
    placed = (
        P("pair", "aux", None),
        P("pair", None, None),
        P("pair", "aux", None, None),
        P("pair", None),
        P(),
        P(),
        P(),
        P("pair"),
    )
    return jax.shard_map(
        on_device,
        mesh=mesh,
        in_specs=placed,
        out_specs=(P("pair", None, None), P("pair")),
        check_vma=False,
    )
```

profile of v0, /device:TPU:0, one launch (start us, length us, event | category | flops | bytes accessed | tf_op | source)
XLA Modules:
  0.0 409.5 jit_solution(2220228275919121516)
XLA Ops:
  7.2 0.8 copy.38
  8.0 0.1 eq.30
  8.1 2.6 copy.57
  10.7 0.2 compare_reduce_fusion.1
  10.9 1.4 convolution_convert_fusion
  12.3 2.2 copy.40
  14.6 6.3 %all-to-all-start = ((bf16[8,256,768]{2,1,0:T(8,128)(2,1)}), bf16[8,256,768]{2,1,0:T(8,128)(2,1)S(1)}, u32[]{:S(2)}, u32[]{:S(2)}) async-start(bf16[8,256,768]{2,1,0:T(8,128)(2,1)} %copy.40), calls=%async_computation | async-start | bytes 6291456 | tf_op jit(solution)/shard_map/all_to_all | solution.py:31
  21.0 0.2 slice_reduce_fusion.1
  21.2 71.2 %all-to-all-done = bf16[8,256,768]{2,1,0:T(8,128)(2,1)S(1)} async-done(((bf16[8,256,768]{2,1,0:T(8,128)(2,1)}), bf16[8,256,768]{2,1,0:T(8,128)(2,1)S(1)}, u32[]{:S(2)}, u32[]{:S(2)}) %all-to-all-start) | async-done | bytes 3145760 | tf_op jit(solution)/shard_map/all_to_all | solution.py:31
  92.4 3.6 gather_fusion.2
  96.0 7.8 %fusion = bf16[16,256,256]{2,1,0:T(8,128)(2,1)} fusion(bf16[16,768,256]{2,1,0:T(8,128)(2,1)} %param.13, bf16[16,256,768]{2,1,0:T(8,128)(2,1)} %gather_fusion.2, pred[16]{0:T(512)(128)(4,1)S(1)} %get-tuple-element.19), kind=kOutput, calls=%fused_computation.8 | convolution fusion | flops 1613758464 | bytes 14680080 | tf_op jit(solution)/shard_map/pav,pvn->pan/dot_general | solution.py:37
  103.8 3.6 gather_fusion.1
  107.4 9.6 %fusion.22 = f32[16,256,256]{2,1,0:T(8,128)} fusion(bf16[16,256,256]{2,1,0:T(8,128)(2,1)} %fusion, bf16[16,768,256]{2,1,0:T(8,128)(2,1)} %param.13, bf16[16,256,768]{2,1,0:T(8,128)(2,1)} %gather_fusion.1, pred[16]{0:T(512)(128)(4,1)S(1)} %get-tuple-element.20), kind=kOutput, calls=%fused_computation.26 | convolution fusion | flops 2151677952 | bytes 18874384 | tf_op jit(solution)/shard_map/pan,pam->pnm/dot_general | solution.py:41
  117.2 0.5 copy-done.2
  117.7 0.7 gather_fusion
  118.5 0.1 select_reduce_fusion
  118.8 50.1 %reduce-scatter.2.cloned.1.call-done = f32[4,256,256]{2,1,0:T(8,128)} async-done(((f32[16,256,256]{2,1,0:T(8,128)}), f32[4,256,256]{2,1,0:T(8,128)}) %reduce-scatter.2.cloned.1.call-update) | async-done | bytes 1048592 | tf_op jit(solution)/shard_map/reduce_scatter | solution.py:49
  168.8 2.3 fusion.60
  171.1 4.9 %all-to-all-start.2 = ((bf16[16,2,256,256]{3,2,1,0:T(8,128)(2,1)}), bf16[16,2,256,256]{3,2,1,0:T(8,128)(2,1)}, u32[]{:S(2)}, u32[]{:S(2)}) async-start(bf16[16,2,256,256]{3,2,1,0:T(8,128)(2,1)} %param.14), calls=%async_computation.3 | async-start | bytes 8388608 | tf_op jit(solution)/shard_map/all_to_all | solution.py:53
  176.2 0.1 copy.42
  176.4 0.3 compare_reduce_fusion
  176.7 64.1 %all-gather.4.cloned.1.call-done = bf16[16,256,256]{2,1,0:T(8,128)(2,1)} async-done(((bf16[4,256,256]{2,1,0:T(8,128)(2,1)}), bf16[16,256,256]{2,1,0:T(8,128)(2,1)}) %all-gather.4.cloned.1.call-update) | async-done | bytes 2097168 | tf_op jit(solution)/shard_map/all_gather | solution.py:68
  240.8 2.8 copy.58
  243.6 0.4 convolution_convert_fusion.2
  244.0 1.2 copy.43
  245.2 4.6 %all-to-all-start.1 = ((bf16[8,256,256]{2,1,0:T(8,128)(2,1)}), bf16[8,256,256]{2,1,0:T(8,128)(2,1)S(1)}, u32[]{:S(2)}, u32[]{:S(2)}) async-start(bf16[8,256,256]{2,1,0:T(8,128)(2,1)} %copy.43), calls=%async_computation.2 | async-start | bytes 2097152 | tf_op jit(solution)/shard_map/all_to_all | solution.py:74
  249.8 0.2 all-gather.6.cloned.1.call-start
  250.0 4.6 %copy.44 = bf16[4,4,2,256,256]{4,3,2,0,1:T(8,128)(2,1)} copy(bf16[4,4,2,256,256]{4,3,2,1,0:T(8,128)(2,1)} %bitcast.3) | data formatting | bytes 8388608 | tf_op jit(solution)/shard_map/all_to_all | solution.py:53
  254.6 21.7 %all-to-all-done.1 = bf16[8,256,256]{2,1,0:T(8,128)(2,1)S(1)} async-done(((bf16[8,256,256]{2,1,0:T(8,128)(2,1)}), bf16[8,256,256]{2,1,0:T(8,128)(2,1)S(1)}, u32[]{:S(2)}, u32[]{:S(2)}) %all-to-all-start.1) | async-done | bytes 1048608 | tf_op jit(solution)/shard_map/all_to_all | solution.py:74
  276.4 2.8 gather_fusion.3
  279.2 5.0 %fusion.14 = bf16[32,256,256]{2,1,0:T(8,128)(2,1)S(1)} fusion(bf16[32,256,256]{2,1,0:T(8,128)(2,1)} %bitcast.56, bf16[32,256,256]{2,1,0:T(8,128)(2,1)} %gather_fusion.3, pred[32]{0:T(512)(128)(4,1)S(1)} %get-tuple-element.6), kind=kOutput, calls=%fused_computation.22 | convolution fusion | flops 1077936128 | bytes 12582944 | tf_op jit(solution)/shard_map/kab,kbc->kac/dot_general | solution.py:78
  284.3 1.6 fusion.39
  285.9 1.7 fusion.62
  287.7 33.3 %all-gather.6.cloned.1.call-done = bf16[16,256,256]{2,1,0:T(8,128)(2,1)} async-done(((bf16[4,256,256]{2,1,0:T(8,128)(2,1)}), bf16[16,256,256]{2,1,0:T(8,128)(2,1)}) %all-gather.6.cloned.1.call-update) | async-done | bytes 2097168 | tf_op jit(solution)/shard_map/all_gather | solution.py:68
  321.1 2.8 copy.59
  323.8 0.4 convolution_convert_fusion.1
  324.3 0.2 copy.47
  324.5 31.0 %all_to_all.33 = bf16[8,256,256]{2,1,0:T(8,128)(2,1)S(1)} all-to-all(bf16[8,256,256]{2,1,0:T(8,128)(2,1)S(1)} %copy.47), channel_id=1, replica_groups=mesh['aux'=4,'pair'=8] {'pair'}, dimensions={0} | all-to-all | bytes 2097152 | tf_op jit(solution)/shard_map/all_to_all | solution.py:74
  355.5 2.8 gather_fusion.4
  358.3 5.0 %fusion.17 = bf16[32,256,256]{2,1,0:T(8,128)(2,1)S(1)} fusion(bf16[32,256,256]{2,1,0:T(8,128)(2,1)} %bitcast.57, bf16[32,256,256]{2,1,0:T(8,128)(2,1)} %gather_fusion.4, pred[32]{0:T(512)(128)(4,1)S(1)} %get-tuple-element.6), kind=kOutput, calls=%fused_computation.23 | convolution fusion | flops 1077936128 | bytes 12582944 | tf_op jit(solution)/shard_map/kab,kbc->kac/dot_general | solution.py:78
  363.3 1.6 fusion.40
  364.9 1.5 multiply_reduce_fusion
  366.4 0.6 dynamic-slice
  367.7 0.2 dynamic-update-slice
  367.9 9.0 %all-reduce = bf16[16]{0:T(256)(128)(2,1)S(1)} all-reduce(bf16[16]{0:T(256)(128)(2,1)S(1)} %dynamic-update-slice), channel_id=1, replica_groups=mesh['aux'=4,'pair'=8] {'aux'}, use_global_device_ids=true, to_apply=%add | all-reduce | flops 16 | bytes 64
  377.0 0.5 convert_element_type.73
  377.5 22.3 %all-gather.8.cloned.1.call-done = bf16[16,256,256]{2,1,0:T(8,128)(2,1)} async-done(((bf16[4,256,256]{2,1,0:T(8,128)(2,1)}), bf16[16,256,256]{2,1,0:T(8,128)(2,1)}) %all-gather.8.cloned.1.call-update) | async-done | bytes 2097168 | tf_op jit(solution)/shard_map/all_gather | solution.py:98
  399.8 3.1 copy.62
  (46 shorter events, 0.9 us)
Async XLA Ops:
  7.2 111.6 %copy-start = (f32[16,256]{1,0:T(8,128)S(1)}, f32[16,256]{1,0:T(8,128)}, u32[]{:S(2)}) copy-start(f32[16,256]{1,0:T(8,128)} %param.15) | copy-start | bytes 49156
  14.6 77.9 %all-to-all-start = ((bf16[8,256,768]{2,1,0:T(8,128)(2,1)}), bf16[8,256,768]{2,1,0:T(8,128)(2,1)S(1)}, u32[]{:S(2)}, u32[]{:S(2)}) async-start(bf16[8,256,768]{2,1,0:T(8,128)(2,1)} %copy.40), calls=%async_computation | async-start | bytes 6291456 | tf_op jit(solution)/shard_map/all_to_all | solution.py:31
  20.9 147.9 %reduce-scatter.2.cloned.1.call-start = ((), (), s32[]{:S(2)}) async-start(), calls=%async_computation.5 | async-start | bytes 5242880 | tf_op jit(solution)/shard_map/reduce_scatter | solution.py:49
  117.0 0.7 copy-start.2
  117.1 123.7 %all-gather.4.cloned.1.call-start = ((), (), s32[]{:S(2)}) async-start(), calls=%async_computation.6 | async-start | bytes 2621440 | tf_op jit(solution)/shard_map/all_gather | solution.py:68
  117.7 0.8 copy-start.7
  171.1 4.9 %copy-start.6 = (s32[128,8]{0,1:T(8,128)S(1)}, s32[128,8]{0,1:T(8,128)}, u32[]{:S(2)}) copy-start(s32[128,8]{0,1:T(8,128)} %param.18) | copy-start | bytes 12292
  171.1 74.0 %all-to-all-start.2 = ((bf16[16,2,256,256]{3,2,1,0:T(8,128)(2,1)}), bf16[16,2,256,256]{3,2,1,0:T(8,128)(2,1)}, u32[]{:S(2)}, u32[]{:S(2)}) async-start(bf16[16,2,256,256]{3,2,1,0:T(8,128)(2,1)} %param.14), calls=%async_computation.3 | async-start | bytes 8388608 | tf_op jit(solution)/shard_map/all_to_all | solution.py:53
  245.2 31.2 %all-to-all-start.1 = ((bf16[8,256,256]{2,1,0:T(8,128)(2,1)}), bf16[8,256,256]{2,1,0:T(8,128)(2,1)S(1)}, u32[]{:S(2)}, u32[]{:S(2)}) async-start(bf16[8,256,256]{2,1,0:T(8,128)(2,1)} %copy.43), calls=%async_computation.2 | async-start | bytes 2097152 | tf_op jit(solution)/shard_map/all_to_all | solution.py:74
  249.8 71.3 %all-gather.6.cloned.1.call-start = ((), (), s32[]{:S(2)}) async-start(), calls=%async_computation.7 | async-start | bytes 2621440 | tf_op jit(solution)/shard_map/all_gather | solution.py:68
  279.2 5.0 %copy-start.3 = (bf16[4,4,2,256,256]{4,3,2,0,1:T(8,128)(2,1)S(1)}, bf16[4,4,2,256,256]{4,3,2,0,1:T(8,128)(2,1)}, u32[]{:S(2)}) copy-start(bf16[4,4,2,256,256]{4,3,2,0,1:T(8,128)(2,1)} %copy.44) | copy-start | bytes 12582916
  279.2 5.1 %copy-start.5 = (f32[4,256,256]{2,1,0:T(8,128)S(1)}, f32[4,256,256]{2,1,0:T(8,128)}, u32[]{:S(2)}) copy-start(f32[4,256,256]{2,1,0:T(8,128)} %reduce-scatter.2.cloned.1.call-done) | copy-start | bytes 3145732
  287.7 112.2 %all-gather.8.cloned.1.call-start = ((), (), s32[]{:S(2)}) async-start(), calls=%async_computation.8 | async-start | bytes 2621440 | tf_op jit(solution)/shard_map/all_gather | solution.py:98
  358.3 5.0 %copy-start.4 = (bf16[4,4,2,256,256]{4,3,2,0,1:T(8,128)(2,1)S(1)}, bf16[4,4,2,256,256]{4,3,2,0,1:T(8,128)(2,1)}, u32[]{:S(2)}) copy-start(bf16[4,4,2,256,256]{4,3,2,0,1:T(8,128)(2,1)} %copy.44) | copy-start | bytes 12582916
  363.3 39.6 %copy-start.1 = (f32[16,256]{1,0:T(8,128)S(1)}, f32[16,256]{1,0:T(8,128)}, u32[]{:S(2)}) copy-start(f32[16,256]{1,0:T(8,128)} %param.15) | copy-start | bytes 49156
  364.9 1.5 copy-start.8
Sparse Core Ops, SparseCore 0:
  117.2 51.6 reduce-scatter.1
  171.4 69.3 all-gather.3
  287.8 33.2 all-gather.5
  366.5 33.2 all-gather.7
where the time goes:
time: 410 us; the launch traced here: 409 us
  waiting for transfers between devices  263 us (64%)
  blocking collectives  40 us (10%)
  matrix products  36.1 us (9%)
  local copies, waits for them, and re-layouts  36 us (9%)
  starting transfers between devices  16.1 us (4%)
  between operations  14.7 us (4%)
    all_gather x2, waiting for transfers between devices, on_device(): cluster_half = lax.all_gather(local_half, 'aux', axis=0, tiled=True)  97.4 us
    all_to_all x1, waiting for transfers between devices, on_device(): lax.all_to_all(outgoing, 'pair', split_axis=0, concat_axis=0, tiled=True)  71.2 us
    reduce_scatter x1, waiting for transfers between devices, on_device(): lax.psum_scatter(partial_coulomb, 'aux', scatter_dimension=0, tiled=True)  50.1 us
    all_to_all x1, blocking collectives, on_device(): lax.all_to_all(outgoing_amps, 'pair', split_axis=0, concat_axis=0, tiled=...  31 us
    all_gather x1, waiting for transfers between devices, on_device(): lax.all_gather(result, 'aux', axis=0, tiled=True)  22.3 us
    all_to_all x1, waiting for transfers between devices, on_device(): lax.all_to_all(outgoing_amps, 'pair', split_axis=0, concat_axis=0, tiled=...  21.7 us
    unnamed x26, local copies, waits for them, and re-layouts  13.4 us
    dot_general x2, matrix products, on_device(): jnp.einsum('kab,kbc->kac', flat_intersections, fetched, preferred_element...  10.1 us
  transfers between devices with their start and end apart: 7, of which 6 were waited for; matrix products, arithmetic and copies ran while one was open for 3% of the time, Pallas kernels for 0%

commit v1 on v0

v1 whole, which is shorter than its diff:
```python
import functools

import jax
import jax.numpy as jnp
from jax import lax
from jax.experimental import pallas as pl
from jax.experimental.pallas import tpu as pltpu
from jax.sharding import PartitionSpec as P

ITERS = 2
CHUNKS = 4
damping = 0.7
BF16 = jnp.bfloat16
F32 = jnp.float32


def dot(x, y, dims):
    return lax.dot_general(x, y, ((dims[:1], dims[1:]), ((), ())), preferred_element_type=F32)


def kernel(
    groups, clusters, table, orbitals, refs, live, occ, slab, energy, maps_hbm, inter_hbm,
    out_hbm, energy_out, *scratch
):
    scratch = list(scratch)

    def take(count):
        got = scratch[:count]
        del scratch[:count]
        return got

    staged, incoming = take(CHUNKS), take(CHUNKS)
    (maps, inter, left, right, part_out, part_in, coulomb, coulomb_half, denom, rden) = take(10)
    (amp, half, energy_row) = take(3)
    split, quarter, zout, zin, fetched = (take(ITERS) for _ in range(5))
    (
        maps_sem, inter_send, inter_recv, slab_send, slab_recv, part_send, part_recv, split_send,
        split_recv, z_send, z_recv, f_send, f_recv, out_send, out_recv, e_send, e_recv,
    ) = scratch

    row = lax.axis_index("aux")
    cluster = lax.axis_index("pair")
    pair_count, virt, width = maps.shape
    share = pair_count // groups
    orb_count = slab.shape[0]
    local_cols = inter.shape[2]
    ref_cols = groups * local_cols
    chunk = slab.shape[1] // CHUNKS
    piece = width // groups

    def remote(src, dst, send, recv, **where):
        return pltpu.make_async_remote_copy(
            src_ref=src, dst_ref=dst, send_sem=send, recv_sem=recv, device_id=where,
            device_id_type=pl.DeviceIdType.MESH,
        )

    def loop(count, body):
        def step(i, carry):
            body(i)
            return carry

        lax.fori_loop(0, count, step, 0)

    def to_pair(i):
        return lax.rem(cluster + i, clusters)

    def from_pair(i):
        return lax.rem(cluster + clusters - i, clusters)

    def to_aux(i):
        return lax.rem(row + i, groups)

    def from_aux(i):
        return lax.rem(row + groups - i, groups)

    def far_first(j):
        return lax.rem(clusters // 2 - 1 + j, clusters - 1) + 1

    barrier = pltpu.get_barrier_semaphore()
    for i in range(1, clusters):
        pl.semaphore_signal(
            barrier, inc=1, device_id={"pair": to_pair(i)}, device_id_type=pl.DeviceIdType.MESH
        )
    for i in range(1, groups):
        pl.semaphore_signal(
            barrier, inc=1, device_id={"aux": to_aux(i)}, device_id_type=pl.DeviceIdType.MESH
        )
    maps_copy = pltpu.make_async_copy(maps_hbm, maps, maps_sem.at[0])
    maps_copy.start()
    inter_own = pltpu.make_async_copy(
        inter_hbm.at[pl.ds(row * share, share)], inter.at[row], maps_sem.at[1]
    )
    inter_own.start()
    pl.semaphore_wait(barrier, clusters + groups - 2)

    def slab_copy(k, i, source):
        return remote(
            staged[k].at[to_pair(i)], incoming[k].at[source], slab_send.at[k, i],
            slab_recv.at[k, i], pair=to_pair(i),
        )

    for k in range(CHUNKS):
        rows = slice(k * chunk, (k + 1) * chunk)

        def send_slab(j, k=k, rows=rows):
            i = far_first(j)
            to = to_pair(i)
            staged[k][to] = slab[table[to], rows, :]
            slab_copy(k, i, cluster).start()

        loop(clusters - 1, send_slab)
        incoming[k][cluster] = slab[table[cluster], rows, :]

    def inter_copy(i, source):
        return remote(
            inter_hbm.at[pl.ds(to_aux(i) * share, share)], inter.at[source], inter_send.at[i],
            inter_recv.at[i], aux=to_aux(i),
        )

    for i in range(1, groups):
        inter_copy(i, row).start()

    def denominators(q):
        p = cluster * pair_count + row * share + q
        occupied = occ[orbitals[2 * p]] + occ[orbitals[2 * p + 1]]
        across = jnp.broadcast_to(energy[row * share + q], (width, width))
        value = across + across.T - occupied
        denom[q] = value
        rden[q] = 1.0 / value

    loop(share, denominators)
    maps_copy.wait()

    def project(k, p):
        first = orbitals[2 * (cluster * pair_count + p)] // orb_count
        second = orbitals[2 * (cluster * pair_count + p) + 1] // orb_count
        both = jnp.concatenate([incoming[k][first], incoming[k][second]], axis=0)
        both = dot(both, maps[p], (1, 0)).astype(BF16)
        rows = slice(k * chunk, (k + 1) * chunk)
        left[p, rows, :] = both[:chunk]
        right[p, rows, :] = both[chunk:]

    def part_copy(i, q):
        return remote(
            part_out.at[i - 1, q], part_in.at[i - 1, q], part_send.at[i, q], part_recv.at[i, q],
            aux=to_aux(i),
        )

    for k in range(CHUNKS):
        loop(clusters - 1, lambda j, k=k: slab_copy(k, far_first(j), from_pair(far_first(j))).wait_recv())
        if k < CHUNKS - 1:
            loop(pair_count, lambda p, k=k: project(k, p))

    last = CHUNKS - 1
    for i in range(1, groups):

        def send_part(q, i=i):
            p = to_aux(i) * share + q
            project(last, p)
            part_out[i - 1, q] = dot(left[p], right[p], (0, 0)).astype(BF16)
            part_copy(i, q).start()

        loop(share, send_part)

    def own_part(q):
        p = row * share + q
        project(last, p)
        coulomb[q] = dot(left[p], right[p], (0, 0))

    loop(share, own_part)

    def split_copy(t, i, source):
        return remote(
            split[t].at[to_aux(i)], quarter[t].at[pl.ds(source * share, share)],
            split_send.at[t, i], split_recv.at[t, i], aux=to_aux(i),
        )

    def z_copy(t, i, source):
        return remote(
            zout[t].at[to_pair(i)], zin[t].at[source], z_send.at[t, i], z_recv.at[t, i],
            pair=to_pair(i),
        )

    def f_copy(t, i, j, member, source):
        return remote(
            zin[t].at[member], fetched[t].at[member, source], f_send.at[t, i, j],
            f_recv.at[t, i, j], aux=to_aux(i),
        )

    def weight(q):
        return live[row * share + q].astype(F32)

    def set_half(t, q, value):
        rounded = value.astype(BF16)
        half[q] = rounded
        for b in range(groups):
            split[t][b, q] = rounded[b * piece:(b + 1) * piece]

    def start_amplitude(q):
        for i in range(1, groups):
            part_copy(i, q).wait_recv()
        total = coulomb[q]
        for i in range(1, groups):
            total = total + part_in[i - 1, q].astype(F32)
        coulomb[q] = total
        coulomb_half[q] = total.astype(BF16)
        value = -weight(q) * total * rden[q]
        amp[q] = value
        set_half(0, q, value)

    loop(share, start_amplitude)

    for t in range(ITERS):
        for i in range(1, groups):
            split_copy(t, i, row).start()

        def keep(q, t=t):
            quarter[t][row * share + q] = split[t][row, q]

        loop(share, keep)

        def quadratic(q):
            product = dot(half[q], coulomb_half[q], (1, 1)).astype(BF16)
            settled = dot(product, half[q], (1, 0)) * (1.0 / width)
            before = amp[q]
            residual = coulomb[q] + denom[q] * before + settled
            amp[q] = before - damping * residual * rden[q]

        for i in range(1, groups):
            split_copy(t, i, from_aux(i)).wait_recv()

        def send_z(j, t=t):
            i = far_first(j)
            to = to_pair(i)
            zout[t][to] = quarter[t][table[clusters + to]]
            z_copy(t, i, cluster).start()

        loop(clusters - 1, send_z)
        mine = quarter[t][table[clusters + cluster]]
        zin[t][cluster] = mine
        fetched[t][cluster, row] = mine
        for i in range(1, groups):
            f_copy(t, i, 0, cluster, row).start()
        loop(share, quadratic)

        def forward(j, t=t):
            j = j + 1
            member = from_pair(j)
            z_copy(t, j, member).wait_recv()
            for i in range(1, groups):
                f_copy(t, i, j, member, row).start()
            fetched[t][member, row] = zin[t][member]

        loop(clusters - 1, forward)
        if t == 0:
            inter_own.wait()
            for i in range(1, groups):
                inter_copy(i, from_aux(i)).wait_recv()

        def arrive(j, t=t):
            for i in range(1, groups):
                f_copy(t, i, j, from_pair(j), from_aux(i)).wait_recv()

        loop(clusters, arrive)

        def update(q, t=t):
            p = cluster * pair_count + row * share + q
            coupled = jnp.zeros((width, width), F32)
            for r in range(ref_cols):
                source = refs[p * ref_cols + r] // pair_count
                overlap = inter[r // local_cols, q, r % local_cols]
                partner = fetched[t][source].reshape(width, width)
                rotated = dot(overlap, partner, (1, 0)).astype(BF16)
                coupled = coupled + dot(rotated, overlap, (1, 1))
            value = weight(q) * (amp[q] + damping * coupled * rden[q])
            if t < ITERS - 1:
                amp[q] = value
                set_half(t + 1, q, value)
            else:
                half[q] = value.astype(BF16)
                for i in range(1, groups):
                    out_copy(i, q, row).start()
                total = jnp.sum(coulomb[q] * value, axis=0, keepdims=True) * weight(q)
                energy_row[q] = total

        def out_copy(i, q, source):
            return remote(
                half.at[q], out_hbm.at[source * share + q], out_send.at[i, q], out_recv.at[i, q],
                aux=to_aux(i),
            )

        loop(share, update)

    out_own = pltpu.make_async_copy(half, out_hbm.at[pl.ds(row * share, share)], maps_sem.at[2])
    out_own.start()

    def e_copy(i, source):
        return remote(
            energy_row, energy_out.at[source], e_send.at[i], e_recv.at[i], aux=to_aux(i)
        )

    for i in range(1, groups):
        e_copy(i, row).start()
    energy_out[row] = energy_row[...]

    for k in range(CHUNKS):
        loop(clusters - 1, lambda j, k=k: slab_copy(k, j + 1, cluster).wait_send())
    for i in range(1, groups):
        inter_copy(i, row).wait_send()
        loop(share, lambda q, i=i: part_copy(i, q).wait_send())
    for t in range(ITERS):
        loop(clusters - 1, lambda j, t=t: z_copy(t, j + 1, cluster).wait_send())
        for i in range(1, groups):
            split_copy(t, i, row).wait_send()
            loop(clusters, lambda j, t=t, i=i: f_copy(t, i, j, from_pair(j), row).wait_send())
    for i in range(1, groups):
        loop(share, lambda q, i=i: out_copy(i, q, row).wait_send())
        loop(share, lambda q, i=i: out_copy(i, q, from_aux(i)).wait_recv())
        e_copy(i, row).wait_send()
        e_copy(i, from_aux(i)).wait_recv()
    out_own.wait()


def on_device(
    orbital_slabs, pno_maps, intersections, pno_energy, occ_energy, pair_orbitals, partners, live
):
    clusters = lax.axis_size("pair")
    groups = lax.axis_size("aux")
    cluster = lax.axis_index("pair")
    orb_count, aux_rows, virt = orbital_slabs.shape
    pair_count, _, width = pno_maps.shape
    cols = intersections.shape[1]
    share = pair_count // groups
    chunk = aux_rows // CHUNKS
    piece = width // groups
    wanted = pair_orbitals.reshape(clusters, -1)
    named = partners.reshape(clusters, -1)
    table = jnp.concatenate([
        jnp.max(jnp.where(wanted // orb_count == cluster, wanted % orb_count, 0), axis=1),
        jnp.max(jnp.where(named // pair_count == cluster, named % pair_count, 0), axis=1),
    ])
    square = (width, width)
    vm = pltpu.VMEM
    dma = lambda *shape: pltpu.SemaphoreType.DMA(shape)
    scratch = (
        [vm((clusters, chunk, virt), BF16)] * (2 * CHUNKS)
        + [
            vm((pair_count, virt, width), BF16),
            vm((groups, share, cols) + square, BF16),
            vm((pair_count, aux_rows, width), BF16),
            vm((pair_count, aux_rows, width), BF16),
            vm((groups - 1, share) + square, BF16),
            vm((groups - 1, share) + square, BF16),
            vm((share,) + square, F32),
            vm((share,) + square, BF16),
            vm((share,) + square, F32),
            vm((share,) + square, F32),
            vm((share,) + square, F32),
            vm((share,) + square, BF16),
            vm((share, 1, width), F32),
        ]
        + [vm((groups, share, piece, width), BF16)] * ITERS
        + [vm((pair_count, piece, width), BF16)] * ITERS
        + [vm((clusters, piece, width), BF16)] * (2 * ITERS)
        + [vm((clusters, groups, piece, width), BF16)] * ITERS
        + [
            dma(3), dma(groups), dma(groups), dma(CHUNKS, clusters), dma(CHUNKS, clusters),
            dma(groups, share), dma(groups, share), dma(ITERS, groups), dma(ITERS, groups),
            dma(ITERS, clusters), dma(ITERS, clusters), dma(ITERS, groups, clusters),
            dma(ITERS, groups, clusters), dma(groups, share), dma(groups, share), dma(groups),
            dma(groups),
        ]
    )
    smem = pl.BlockSpec(memory_space=pltpu.SMEM)
    vmem = pl.BlockSpec(memory_space=pltpu.VMEM)
    anywhere = pl.BlockSpec(memory_space=pl.ANY)
    result, energy = pl.pallas_call(
        functools.partial(kernel, groups, clusters),
        out_shape=(
            jax.ShapeDtypeStruct((pair_count,) + square, BF16),
            jax.ShapeDtypeStruct((groups, share, 1, width), F32),
        ),
        in_specs=[smem] * 5 + [vmem, vmem, anywhere, anywhere],
        out_specs=(anywhere, vmem),
        scratch_shapes=scratch,
        compiler_params=pltpu.CompilerParams(
            collective_id=0, has_side_effects=True, vmem_limit_bytes=62 << 20
        ),
        name="local_pair_amplitudes",
    )(
        table, pair_orbitals.reshape(-1), partners.reshape(-1), live, occ_energy, orbital_slabs,
        pno_energy.reshape(pair_count, 1, width), pno_maps, intersections,
    )
    return result, jnp.sum(energy, axis=(2, 3)).reshape(-1)


def solution(mesh):
    placed = (
        P("pair", "aux", None),
        P("pair", None, None),
        P("pair", "aux", None, None),
        P("pair", None),
        P(),
        P(),
        P(),
        P("pair"),
    )
    return jax.shard_map(
        on_device,
        mesh=mesh,
        in_specs=placed,
        out_specs=(P("pair", None, None), P("pair")),
        check_vma=False,
    )
```

time: 410 us -> 192 us (0.47)
  waiting for transfers between devices: 263 us -> 0 us
  Pallas kernels: 0 us -> 179 us
  blocking collectives: 40 us -> 0 us
  matrix products: 36.1 us -> 0 us
  local copies, waits for them, and re-layouts: 36 us -> 8.17 us
  starting transfers between devices: 16.1 us -> 0 us
  between operations: 14.7 us -> 0.65 us
    pallas_call x0 -> x1, Pallas kernels: none -> 179 us  [on_device(): pl.pallas_call(functools.partial(kernel, groups, clusters), out_shape=(ja...]
    all_gather x3 -> x0, waiting for transfers between devices: 120 us -> none  [the longest x2 97.4 us: on_device(): cluster_half = lax.all_gather(local_half, 'aux', axis=0, tiled=True)]
    all_to_all x3 -> x0, waiting for transfers between devices: 93 us -> none  [the longest x1 71.2 us: on_device(): lax.all_to_all(outgoing, 'pair', split_axis=0, concat_axis=0, tiled=True)]
    reduce_scatter x1 -> x0, waiting for transfers between devices: 50.1 us -> none  [on_device(): lax.psum_scatter(partial_coulomb, 'aux', scatter_dimension=0, tiled=True)]
    dot_general x11 -> x0, matrix products: 36.1 us -> none  [the longest x2 10.1 us: on_device(): jnp.einsum('kab,kbc->kac', flat_intersections, fetched, preferred_element...]
    all_to_all x1 -> x0, blocking collectives: 31 us -> none  [on_device(): lax.all_to_all(outgoing_amps, 'pair', split_axis=0, concat_axis=0, tiled=...]
    all_to_all x3 -> x0, starting transfers between devices: 15.8 us -> none  [the longest x1 6.32 us: on_device(): lax.all_to_all(outgoing, 'pair', split_axis=0, concat_axis=0, tiled=True)]
    gather x6 -> x0, local copies, waits for them, and re-layouts: 13.6 us -> none  [the longest x2 5.62 us: on_device(): jnp.take(lax.all_to_all(outgoing_amps, 'pair', split_axis=0, concat_axis=...]
  transfers between devices with their start and end apart: 7 -> 0, of which waited for: 6 -> 0; matrix products, arithmetic and copies ran while one was open for 3% -> 0% of each run, Pallas kernels for 0% -> 0%
where the time goes in v1:
time: 192 us; the launch traced here: 191 us
  Pallas kernels  179 us (93%)
  local copies, waits for them, and re-layouts  8.17 us (4%)
  other arithmetic  3.09 us (2%)
    pallas_call x1, Pallas kernels, on_device(): pl.pallas_call(functools.partial(kernel, groups, clusters), out_shape=(ja...  179 us
    unnamed x3, local copies, waits for them, and re-layouts  4.66 us

profile of v1, /device:TPU:0, one launch (start us, length us, event | category | flops | bytes accessed | tf_op | source)
XLA Modules:
  0.0 191.2 jit_solution(11430324483030301481)
XLA Ops:
  0.6 0.7 fusion.5
  1.3 0.7 fusion.2
  2.0 0.1 reduce_max.36
  2.1 0.1 reduce_max.37
  2.2 0.1 reduce_max.24
  2.3 0.1 reduce_max.25
  2.5 0.6 pad_add_fusion.table
  3.0 1.3 reshape.22.energy
  4.4 0.8 copy.10
  5.2 0.7 reshape.20.orbitals
  5.9 0.8 copy.11
  6.7 0.7 reshape.21.refs
  7.4 179.3 %local_pair_amplitudes.1 = (bf16[16,256,256]{2,1,0:T(8,128)(2,1)}, f32[4,4,1,256]{3,2,1,0:T(1,128)}) custom-call(s32[16]{0:T(128)} %pad_add_fusion.table, s32[256]{0:T(256)} %reshape.20.orbitals, s32[1024]{0:T(1024)} %reshape.21.refs, s32[16]{0:T(128)} %live.1, f32[32]{0:T(128)} %occ.1, bf16[4,256,768]{2,1,0:T(8,128)(2,1)} %slab.1, ...), custom_call_target="tpu_custom_call" | custom-call | tf_op jit(solution)/shard_map/local_pair_amplitudes/pallas_call | solution.py:377
  186.7 0.8 reduce_sum.9
  187.5 0.6 reshape.23
  188.1 3.1 %copy.13 = bf16[16,256,256]{2,1,0:T(8,128)(2,1)} copy(bf16[16,256,256]{2,1,0:T(8,128)(2,1)} %get-tuple-element.8) | data formatting | bytes 4194304

commit v2 on v1

--- a/solution.py
+++ b/solution.py
@@ -8,7 +8,9 @@
 from jax.sharding import PartitionSpec as P
 
 ITERS = 2
-CHUNKS = 4
+PARTS = (5, 5, 3, 3)
+CHUNKS = len(PARTS)
+HEAD = 2
 damping = 0.7
 BF16 = jnp.bfloat16
 F32 = jnp.float32
@@ -19,7 +21,7 @@
 
 
 def kernel(
-    groups, clusters, table, orbitals, refs, live, occ, slab, energy, maps_hbm, inter_hbm,
+    groups, clusters, orbitals, refs, live, occ, slab, energy, maps_hbm, inter_hbm,
     out_hbm, energy_out, *scratch
 ):
     scratch = list(scratch)
@@ -30,11 +32,13 @@
         return got
 
     staged, incoming = take(CHUNKS), take(CHUNKS)
-    (maps, inter, left, right, part_out, part_in, coulomb, coulomb_half, denom, rden) = take(10)
+    tail_out, tail_in = take(CHUNKS - HEAD), take(CHUNKS - HEAD)
+    (table, maps, inter, left, right, part_out, part_in, coulomb, coulomb_half, denom, rden) = take(11)
     (amp, half, energy_row) = take(3)
-    split, quarter, zout, zin, fetched = (take(ITERS) for _ in range(5))
+    split, quarter, zout, zin = (take(ITERS) for _ in range(4))
+    (fetched,) = take(1)
     (
-        maps_sem, inter_send, inter_recv, slab_send, slab_recv, part_send, part_recv, split_send,
+        maps_sem, inter_send, inter_recv, slab_send, slab_recv, part_send, part_recv, tail_send, tail_recv, split_send,
         split_recv, z_send, z_recv, f_send, f_recv, out_send, out_recv, e_send, e_recv,
     ) = scratch
 
@@ -45,7 +49,8 @@
     orb_count = slab.shape[0]
     local_cols = inter.shape[2]
     ref_cols = groups * local_cols
-    chunk = slab.shape[1] // CHUNKS
+    unit = slab.shape[1] // sum(PARTS)
+    starts = [sum(PARTS[:k]) * unit for k in range(CHUNKS + 1)]
     piece = width // groups
 
     def remote(src, dst, send, recv, **where):
@@ -91,6 +96,24 @@
         inter_hbm.at[pl.ds(row * share, share)], inter.at[row], maps_sem.at[1]
     )
     inter_own.start()
+
+    def scan_orbitals(c):
+        found = 0
+        for n in range(pair_count):
+            for side in range(2):
+                at = orbitals[side, c * pair_count + n] - cluster * orb_count
+                found = jnp.where((at >= 0) & (at < orb_count), at, found)
+        table[c] = found
+
+    def scan_pairs(c):
+        found = 0
+        for n in range(pair_count):
+            for r in range(ref_cols):
+                at = refs[r, c * pair_count + n] - cluster * pair_count
+                found = jnp.where((at >= 0) & (at < pair_count), at, found)
+        table[clusters + c] = found
+
+    loop(clusters, scan_orbitals)
     pl.semaphore_wait(barrier, clusters + groups - 2)
 
     def slab_copy(k, i, source):
@@ -100,7 +123,7 @@
         )
 
     for k in range(CHUNKS):
-        rows = slice(k * chunk, (k + 1) * chunk)
+        rows = slice(starts[k], starts[k + 1])
 
         def send_slab(j, k=k, rows=rows):
             i = far_first(j)
@@ -122,23 +145,27 @@
 
     def denominators(q):
         p = cluster * pair_count + row * share + q
-        occupied = occ[orbitals[2 * p]] + occ[orbitals[2 * p + 1]]
-        across = jnp.broadcast_to(energy[row * share + q], (width, width))
+        occupied = occ[orbitals[0, p]] + occ[orbitals[1, p]]
+        across = jnp.broadcast_to(energy[pl.ds(row * share + q, 1), :], (width, width))
         value = across + across.T - occupied
         denom[q] = value
         rden[q] = 1.0 / value
 
     loop(share, denominators)
+    loop(clusters, scan_pairs)
     maps_copy.wait()
 
     def project(k, p):
-        first = orbitals[2 * (cluster * pair_count + p)] // orb_count
-        second = orbitals[2 * (cluster * pair_count + p) + 1] // orb_count
+        first = orbitals[0, cluster * pair_count + p] // orb_count
+        second = orbitals[1, cluster * pair_count + p] // orb_count
         both = jnp.concatenate([incoming[k][first], incoming[k][second]], axis=0)
-        both = dot(both, maps[p], (1, 0)).astype(BF16)
-        rows = slice(k * chunk, (k + 1) * chunk)
-        left[p, rows, :] = both[:chunk]
-        right[p, rows, :] = both[chunk:]
+        return dot(both, maps[p], (1, 0)).astype(BF16)
+
+    def project_head(k, p):
+        both = project(k, p)
+        count = starts[k + 1] - starts[k]
+        left[p, starts[k]:starts[k + 1], :] = both[:count]
+        right[p, starts[k]:starts[k + 1], :] = both[count:]
 
     def part_copy(i, q):
         return remote(
@@ -146,33 +173,41 @@
             aux=to_aux(i),
         )
 
+    def tail_copy(k, i, q):
+        return remote(
+            tail_out[k - HEAD].at[i - 1, q], tail_in[k - HEAD].at[i, q],
+            tail_send.at[k - HEAD, i, q], tail_recv.at[k - HEAD, i, q], aux=to_aux(i),
+        )
+
+    def send_part(q):
+        for i in range(1, groups):
+            p = to_aux(i) * share + q
+            project_head(HEAD - 1, p)
+            part_out[i - 1, q] = dot(left[p], right[p], (0, 0)).astype(BF16)
+            part_copy(i, q).start()
+        p = row * share + q
+        project_head(HEAD - 1, p)
+        coulomb[q] = dot(left[p], right[p], (0, 0))
+
+    def send_tail(k, q):
+        for i in range(1, groups):
+            tail_out[k - HEAD][i - 1, q] = project(k, to_aux(i) * share + q)
+            tail_copy(k, i, q).start()
+        tail_in[k - HEAD][0, q] = project(k, row * share + q)
+
     for k in range(CHUNKS):
         loop(clusters - 1, lambda j, k=k: slab_copy(k, far_first(j), from_pair(far_first(j))).wait_recv())
-        if k < CHUNKS - 1:
-            loop(pair_count, lambda p, k=k: project(k, p))
-
-    last = CHUNKS - 1
-    for i in range(1, groups):
-
-        def send_part(q, i=i):
-            p = to_aux(i) * share + q
-            project(last, p)
-            part_out[i - 1, q] = dot(left[p], right[p], (0, 0)).astype(BF16)
-            part_copy(i, q).start()
-
-        loop(share, send_part)
-
-    def own_part(q):
-        p = row * share + q
-        project(last, p)
-        coulomb[q] = dot(left[p], right[p], (0, 0))
-
-    loop(share, own_part)
-
-    def split_copy(t, i, source):
-        return remote(
-            split[t].at[to_aux(i)], quarter[t].at[pl.ds(source * share, share)],
-            split_send.at[t, i], split_recv.at[t, i], aux=to_aux(i),
+        if k < HEAD - 1:
+            loop(pair_count, lambda p, k=k: project_head(k, p))
+        elif k == HEAD - 1:
+            loop(share, send_part)
+        else:
+            loop(share, lambda q, k=k: send_tail(k, q))
+
+    def split_copy(t, i, q, source):
+        return remote(
+            split[t].at[to_aux(i), q], quarter[t].at[source * share + q],
+            split_send.at[t, i, q], split_recv.at[t, i, q], aux=to_aux(i),
         )
 
     def z_copy(t, i, source):
@@ -183,7 +218,7 @@
 
     def f_copy(t, i, j, member, source):
         return remote(
-            zin[t].at[member], fetched[t].at[member, source], f_send.at[t, i, j],
+            zin[t].at[member], fetched.at[member, source], f_send.at[t, i, j],
             f_recv.at[t, i, j], aux=to_aux(i),
         )
 
@@ -195,6 +230,9 @@
         half[q] = rounded
         for b in range(groups):
             split[t][b, q] = rounded[b * piece:(b + 1) * piece]
+        for i in range(1, groups):
+            split_copy(t, i, q, row).start()
+        quarter[t][row * share + q] = split[t][row, q]
 
     def start_amplitude(q):
         for i in range(1, groups):
@@ -202,6 +240,15 @@
         total = coulomb[q]
         for i in range(1, groups):
             total = total + part_in[i - 1, q].astype(F32)
+        lefts, rights = [], []
+        for k in range(HEAD, CHUNKS):
+            count = starts[k + 1] - starts[k]
+            for i in range(groups):
+                if i:
+                    tail_copy(k, i, q).wait_recv()
+                lefts.append(tail_in[k - HEAD][i, q, :count, :])
+                rights.append(tail_in[k - HEAD][i, q, count:, :])
+        total = total + dot(jnp.concatenate(lefts, 0), jnp.concatenate(rights, 0), (0, 0))
         coulomb[q] = total
         coulomb_half[q] = total.astype(BF16)
         value = -weight(q) * total * rden[q]
@@ -211,14 +258,6 @@
     loop(share, start_amplitude)
 
     for t in range(ITERS):
-        for i in range(1, groups):
-            split_copy(t, i, row).start()
-
-        def keep(q, t=t):
-            quarter[t][row * share + q] = split[t][row, q]
-
-        loop(share, keep)
-
         def quadratic(q):
             product = dot(half[q], coulomb_half[q], (1, 1)).astype(BF16)
             settled = dot(product, half[q], (1, 0)) * (1.0 / width)
@@ -227,7 +266,7 @@
             amp[q] = before - damping * residual * rden[q]
 
         for i in range(1, groups):
-            split_copy(t, i, from_aux(i)).wait_recv()
+            loop(share, lambda q, t=t, i=i: split_copy(t, i, q, from_aux(i)).wait_recv())
 
         def send_z(j, t=t):
             i = far_first(j)
@@ -238,7 +277,7 @@
         loop(clusters - 1, send_z)
         mine = quarter[t][table[clusters + cluster]]
         zin[t][cluster] = mine
-        fetched[t][cluster, row] = mine
+        fetched[cluster, row] = mine
         for i in range(1, groups):
             f_copy(t, i, 0, cluster, row).start()
         loop(share, quadratic)
@@ -249,7 +288,7 @@
             z_copy(t, j, member).wait_recv()
             for i in range(1, groups):
                 f_copy(t, i, j, member, row).start()
-            fetched[t][member, row] = zin[t][member]
+            fetched[member, row] = zin[t][member]
 
         loop(clusters - 1, forward)
         if t == 0:
@@ -267,13 +306,14 @@
             p = cluster * pair_count + row * share + q
             coupled = jnp.zeros((width, width), F32)
             for r in range(ref_cols):
-                source = refs[p * ref_cols + r] // pair_count
+                source = refs[r, p] // pair_count
                 overlap = inter[r // local_cols, q, r % local_cols]
-                partner = fetched[t][source].reshape(width, width)
+                partner = fetched[source].reshape(width, width)
                 rotated = dot(overlap, partner, (1, 0)).astype(BF16)
                 coupled = coupled + dot(rotated, overlap, (1, 1))
-            value = weight(q) * (amp[q] + damping * coupled * rden[q])
+            value = amp[q] + damping * coupled * rden[q]
             if t < ITERS - 1:
+                value = weight(q) * value
                 amp[q] = value
                 set_half(t + 1, q, value)
             else:
@@ -296,22 +336,24 @@
 
     def e_copy(i, source):
         return remote(
-            energy_row, energy_out.at[source], e_send.at[i], e_recv.at[i], aux=to_aux(i)
+            energy_row, energy_out.at[pl.ds(source * share, share)], e_send.at[i], e_recv.at[i], aux=to_aux(i)
         )
 
     for i in range(1, groups):
         e_copy(i, row).start()
-    energy_out[row] = energy_row[...]
+    energy_out[pl.ds(row * share, share)] = energy_row[...]
 
     for k in range(CHUNKS):
         loop(clusters - 1, lambda j, k=k: slab_copy(k, j + 1, cluster).wait_send())
     for i in range(1, groups):
         inter_copy(i, row).wait_send()
         loop(share, lambda q, i=i: part_copy(i, q).wait_send())
+        for k in range(HEAD, CHUNKS):
+            loop(share, lambda q, i=i, k=k: tail_copy(k, i, q).wait_send())
     for t in range(ITERS):
         loop(clusters - 1, lambda j, t=t: z_copy(t, j + 1, cluster).wait_send())
         for i in range(1, groups):
-            split_copy(t, i, row).wait_send()
+            loop(share, lambda q, t=t, i=i: split_copy(t, i, q, row).wait_send())
             loop(clusters, lambda j, t=t, i=i: f_copy(t, i, j, from_pair(j), row).wait_send())
     for i in range(1, groups):
         loop(share, lambda q, i=i: out_copy(i, q, row).wait_send())
@@ -326,29 +368,27 @@
 ):
     clusters = lax.axis_size("pair")
     groups = lax.axis_size("aux")
-    cluster = lax.axis_index("pair")
-    orb_count, aux_rows, virt = orbital_slabs.shape
+    _, aux_rows, virt = orbital_slabs.shape
     pair_count, _, width = pno_maps.shape
     cols = intersections.shape[1]
     share = pair_count // groups
-    chunk = aux_rows // CHUNKS
+    unit = aux_rows // sum(PARTS)
+    head_rows = sum(PARTS[:HEAD]) * unit
+    tails = [2 * part * unit for part in PARTS[HEAD:]]
     piece = width // groups
-    wanted = pair_orbitals.reshape(clusters, -1)
-    named = partners.reshape(clusters, -1)
-    table = jnp.concatenate([
-        jnp.max(jnp.where(wanted // orb_count == cluster, wanted % orb_count, 0), axis=1),
-        jnp.max(jnp.where(named // pair_count == cluster, named % pair_count, 0), axis=1),
-    ])
     square = (width, width)
     vm = pltpu.VMEM
     dma = lambda *shape: pltpu.SemaphoreType.DMA(shape)
     scratch = (
-        [vm((clusters, chunk, virt), BF16)] * (2 * CHUNKS)
+        [vm((clusters, part * unit, virt), BF16) for part in PARTS] * 2
+        + [vm((groups - 1, share, rows, width), BF16) for rows in tails]
+        + [vm((groups, share, rows, width), BF16) for rows in tails]
         + [
+            pltpu.SMEM((2 * clusters,), jnp.int32),
             vm((pair_count, virt, width), BF16),
             vm((groups, share, cols) + square, BF16),
-            vm((pair_count, aux_rows, width), BF16),
-            vm((pair_count, aux_rows, width), BF16),
+            vm((pair_count, head_rows, width), BF16),
+            vm((pair_count, head_rows, width), BF16),
             vm((groups - 1, share) + square, BF16),
             vm((groups - 1, share) + square, BF16),
             vm((share,) + square, F32),
@@ -362,10 +402,11 @@
         + [vm((groups, share, piece, width), BF16)] * ITERS
         + [vm((pair_count, piece, width), BF16)] * ITERS
         + [vm((clusters, piece, width), BF16)] * (2 * ITERS)
-        + [vm((clusters, groups, piece, width), BF16)] * ITERS
+        + [vm((clusters, groups, piece, width), BF16)]
         + [
             dma(3), dma(groups), dma(groups), dma(CHUNKS, clusters), dma(CHUNKS, clusters),
-            dma(groups, share), dma(groups, share), dma(ITERS, groups), dma(ITERS, groups),
+            dma(groups, share), dma(groups, share), dma(CHUNKS - HEAD, groups, share),
+            dma(CHUNKS - HEAD, groups, share), dma(ITERS, groups, share), dma(ITERS, groups, share),
             dma(ITERS, clusters), dma(ITERS, clusters), dma(ITERS, groups, clusters),
             dma(ITERS, groups, clusters), dma(groups, share), dma(groups, share), dma(groups),
             dma(groups),
@@ -378,9 +419,9 @@
         functools.partial(kernel, groups, clusters),
         out_shape=(
             jax.ShapeDtypeStruct((pair_count,) + square, BF16),
-            jax.ShapeDtypeStruct((groups, share, 1, width), F32),
+            jax.ShapeDtypeStruct((pair_count, 1, width), F32),
         ),
-        in_specs=[smem] * 5 + [vmem, vmem, anywhere, anywhere],
+        in_specs=[smem] * 4 + [vmem, vmem, anywhere, anywhere],
         out_specs=(anywhere, vmem),
         scratch_shapes=scratch,
         compiler_params=pltpu.CompilerParams(
@@ -388,10 +429,11 @@
         ),
         name="local_pair_amplitudes",
     )(
-        table, pair_orbitals.reshape(-1), partners.reshape(-1), live, occ_energy, orbital_slabs,
-        pno_energy.reshape(pair_count, 1, width), pno_maps, intersections,
+        pair_orbitals.T, partners.T, live, occ_energy, orbital_slabs, pno_energy, pno_maps,
+        intersections,
     )
-    return result, jnp.sum(energy, axis=(2, 3)).reshape(-1)
+    result = jnp.where(live[:, None, None] > 0, result, jnp.zeros_like(result))
+    return result, jnp.sum(energy, axis=(1, 2))
 
 
 def solution(mesh):

time: 192 us -> 183 us (0.953)
  local copies, waits for them, and re-layouts: 8.17 us -> 0.01 us
  Pallas kernels: 179 us -> 177 us
    unnamed x3 -> x2, local copies, waits for them, and re-layouts: 4.66 us -> 0.01 us
    reshape x4 -> x0, local copies, waits for them, and re-layouts: 3.35 us -> none  [the longest x1 1.33 us: on_device(): pno_energy.reshape(pair_count, 1, width)]
    select_n x0 -> x1, other arithmetic: none -> 3.12 us  [on_device(): result = jnp.where(live[:, None, None] > 0, result, jnp.zeros_like(result))]
where the time goes in v2:
time: 183 us
  Pallas kernels  177 us (97%)
  other arithmetic  4.5 us (2%)
    pallas_call x1, Pallas kernels, on_device(): pl.pallas_call(functools.partial(kernel, groups, clusters), out_shape=(ja...  177 us

profile of v2, /device:TPU:0, one launch (start us, length us, event | category | flops | bytes accessed | tf_op | source)
XLA Modules:
  0.0 182.6 jit_solution(16614188635465020)
XLA Ops:
  0.6 0.7 broadcast_compare_fusion
  1.3 177.5 %local_pair_amplitudes.1 = (bf16[16,256,256]{2,1,0:T(8,128)(2,1)}, f32[16,1,256]{2,1,0:T(1,128)}) custom-call(s32[2,128]{1,0:T(2,128)} %bitcast.3, s32[8,128]{1,0:T(8,128)} %bitcast.2, s32[16]{0:T(128)} %live.1, f32[32]{0:T(128)} %occ.1, bf16[4,256,768]{2,1,0:T(8,128)(2,1)} %slab.1, f32[16,256]{1,0:T(8,128)} %energy.1, bf16[16,768,256]{2,1,0:T(8,128)(2,1)} %maps_hbm.1, ...), custom_call_target="tpu_custom_call" | custom-call | tf_op jit(solution)/shard_map/local_pair_amplitudes/pallas_call | solution.py:418
  178.8 0.0 copy-start
  178.8 3.1 %broadcast_select_fusion = bf16[16,256,256]{2,1,0:T(8,128)(2,1)} fusion(bf16[16,256,256]{2,1,0:T(8,128)(2,1)} %get-tuple-element.4, pred[16]{0:T(512)(128)(4,1)S(1)} %broadcast_compare_fusion), kind=kLoop, calls=%fused_computation | loop fusion | flops 1048576 | bytes 4194320 | tf_op jit(solution)/shard_map/jit(_where)/select_n | solution.py:435
  181.9 0.0 copy-done
  181.9 0.7 reduce_sum.9
Async XLA Ops:
  178.8 3.1 %copy-start = (f32[16,1,256]{2,1,0:T(1,128)S(1)}, f32[16,1,256]{2,1,0:T(1,128)}, u32[]{:S(2)}) copy-start(f32[16,1,256]{2,1,0:T(1,128)} %get-tuple-element.5) | copy-start | bytes 49156

commit v3 on v2

--- a/solution.py
+++ b/solution.py
@@ -122,26 +122,39 @@
             slab_recv.at[k, i], pair=to_pair(i),
         )
 
-    for k in range(CHUNKS):
+    def inter_copy(i, q, source):
+        return remote(
+            inter_hbm.at[to_aux(i) * share + q], inter.at[source, q], inter_send.at[i, q],
+            inter_recv.at[i, q], aux=to_aux(i),
+        )
+
+    window = (clusters - 1) // 2
+
+    def issue(k):
         rows = slice(starts[k], starts[k + 1])
-
-        def send_slab(j, k=k, rows=rows):
+        pairs = range(k * share // HEAD, (k + 1) * share // HEAD) if k < HEAD else ()
+
+        def send_slab(j):
             i = far_first(j)
             to = to_pair(i)
             staged[k][to] = slab[table[to], rows, :]
             slab_copy(k, i, cluster).start()
 
-        loop(clusters - 1, send_slab)
+        loop(window, send_slab)
+        for n, q in enumerate(pairs):
+            for i in range(1, groups):
+                inter_copy(i, q, row).start()
+            if n == 0:
+                loop(clusters - 1 - window, lambda j: send_slab(j + window))
+        if not pairs:
+            loop(clusters - 1 - window, lambda j: send_slab(j + window))
         incoming[k][cluster] = slab[table[cluster], rows, :]
 
-    def inter_copy(i, source):
-        return remote(
-            inter_hbm.at[pl.ds(to_aux(i) * share, share)], inter.at[source], inter_send.at[i],
-            inter_recv.at[i], aux=to_aux(i),
-        )
-
-    for i in range(1, groups):
-        inter_copy(i, row).start()
+    def issue_after(k):
+        loop(window, lambda j: slab_copy(k, far_first(j), cluster).wait_send())
+        issue(k + 1)
+
+    issue(0)
 
     def denominators(q):
         p = cluster * pair_count + row * share + q
@@ -154,6 +167,7 @@
     loop(share, denominators)
     loop(clusters, scan_pairs)
     maps_copy.wait()
+    issue_after(0)
 
     def project(k, p):
         first = orbitals[0, cluster * pair_count + p] // orb_count
@@ -197,6 +211,8 @@
 
     for k in range(CHUNKS):
         loop(clusters - 1, lambda j, k=k: slab_copy(k, far_first(j), from_pair(far_first(j))).wait_recv())
+        if 0 < k + 1 < CHUNKS - 1:
+            issue_after(k + 1)
         if k < HEAD - 1:
             loop(pair_count, lambda p, k=k: project_head(k, p))
         elif k == HEAD - 1:
@@ -294,7 +310,7 @@
         if t == 0:
             inter_own.wait()
             for i in range(1, groups):
-                inter_copy(i, from_aux(i)).wait_recv()
+                loop(share, lambda q, i=i: inter_copy(i, q, from_aux(i)).wait_recv())
 
         def arrive(j, t=t):
             for i in range(1, groups):
@@ -312,15 +328,15 @@
                 rotated = dot(overlap, partner, (1, 0)).astype(BF16)
                 coupled = coupled + dot(rotated, overlap, (1, 1))
             value = amp[q] + damping * coupled * rden[q]
+            value = weight(q) * value
             if t < ITERS - 1:
-                value = weight(q) * value
                 amp[q] = value
                 set_half(t + 1, q, value)
             else:
                 half[q] = value.astype(BF16)
                 for i in range(1, groups):
                     out_copy(i, q, row).start()
-                total = jnp.sum(coulomb[q] * value, axis=0, keepdims=True) * weight(q)
+                total = jnp.sum(coulomb[q] * value, axis=0, keepdims=True)
                 energy_row[q] = total
 
         def out_copy(i, q, source):
@@ -344,9 +360,13 @@
     energy_out[pl.ds(row * share, share)] = energy_row[...]
 
     for k in range(CHUNKS):
-        loop(clusters - 1, lambda j, k=k: slab_copy(k, j + 1, cluster).wait_send())
+        done = window if k < CHUNKS - 1 else 0
+        loop(
+            clusters - 1 - done,
+            lambda j, k=k, done=done: slab_copy(k, far_first(j + done), cluster).wait_send(),
+        )
     for i in range(1, groups):
-        inter_copy(i, row).wait_send()
+        loop(share, lambda q, i=i: inter_copy(i, q, row).wait_send())
         loop(share, lambda q, i=i: part_copy(i, q).wait_send())
         for k in range(HEAD, CHUNKS):
             loop(share, lambda q, i=i, k=k: tail_copy(k, i, q).wait_send())
@@ -404,7 +424,7 @@
         + [vm((clusters, piece, width), BF16)] * (2 * ITERS)
         + [vm((clusters, groups, piece, width), BF16)]
         + [
-            dma(3), dma(groups), dma(groups), dma(CHUNKS, clusters), dma(CHUNKS, clusters),
+            dma(3), dma(groups, share), dma(groups, share), dma(CHUNKS, clusters), dma(CHUNKS, clusters),
             dma(groups, share), dma(groups, share), dma(CHUNKS - HEAD, groups, share),
             dma(CHUNKS - HEAD, groups, share), dma(ITERS, groups, share), dma(ITERS, groups, share),
             dma(ITERS, clusters), dma(ITERS, clusters), dma(ITERS, groups, clusters),
@@ -432,7 +452,6 @@
         pair_orbitals.T, partners.T, live, occ_energy, orbital_slabs, pno_energy, pno_maps,
         intersections,
     )
-    result = jnp.where(live[:, None, None] > 0, result, jnp.zeros_like(result))
     return result, jnp.sum(energy, axis=(1, 2))
 
 

time: 183 us -> 186 us (1.016)
  local copies, waits for them, and re-layouts: 0.01 us -> 3.09 us
  other arithmetic: 4.5 us -> 1.43 us
  Pallas kernels: 177 us -> 180 us
    select_n x1 -> x0, other arithmetic: 3.12 us -> none  [on_device(): result = jnp.where(live[:, None, None] > 0, result, jnp.zeros_like(result))]
    unnamed x2 -> x1, local copies, waits for them, and re-layouts: 0.01 us -> 3.09 us
    pallas_call x1, Pallas kernels: 177 us -> 180 us  [on_device(): pl.pallas_call(functools.partial(kernel, groups, clusters), out_shape=(ja...]
where the time goes in v3:
time: 186 us; the launch traced here: 185 us
  Pallas kernels  180 us (97%)
  local copies, waits for them, and re-layouts  3.09 us (2%)
    pallas_call x1, Pallas kernels, on_device(): pl.pallas_call(functools.partial(kernel, groups, clusters), out_shape=(ja...  180 us

profile of v3, /device:TPU:0, one launch (start us, length us, event | category | flops | bytes accessed | tf_op | source)
XLA Modules:
  0.0 185.4 jit_solution(2296603260323608725)
XLA Ops:
  0.6 180.2 %local_pair_amplitudes.1 = (bf16[16,256,256]{2,1,0:T(8,128)(2,1)}, f32[16,1,256]{2,1,0:T(1,128)}) custom-call(s32[2,128]{1,0:T(2,128)} %bitcast.3, s32[8,128]{1,0:T(8,128)} %bitcast.2, s32[16]{0:T(128)} %live.1, f32[32]{0:T(128)} %occ.1, bf16[4,256,768]{2,1,0:T(8,128)(2,1)} %slab.1, f32[16,256]{1,0:T(8,128)} %energy.1, bf16[16,768,256]{2,1,0:T(8,128)(2,1)} %maps_hbm.1, ...), custom_call_target="tpu_custom_call" | custom-call | tf_op jit(solution)/shard_map/local_pair_amplitudes/pallas_call | solution.py:438
  180.8 1.4 reduce_sum.9
  182.3 3.1 %copy.11 = bf16[16,256,256]{2,1,0:T(8,128)(2,1)} copy(bf16[16,256,256]{2,1,0:T(8,128)(2,1)} %get-tuple-element.8) | data formatting | bytes 4194304

commit v4 on v2

--- a/solution.py
+++ b/solution.py
@@ -8,7 +8,7 @@
 from jax.sharding import PartitionSpec as P
 
 ITERS = 2
-PARTS = (5, 5, 3, 3)
+PARTS = (6, 6, 4)
 CHUNKS = len(PARTS)
 HEAD = 2
 damping = 0.7
@@ -39,7 +39,7 @@
     (fetched,) = take(1)
     (
         maps_sem, inter_send, inter_recv, slab_send, slab_recv, part_send, part_recv, tail_send, tail_recv, split_send,
-        split_recv, z_send, z_recv, f_send, f_recv, out_send, out_recv, e_send, e_recv,
+        split_recv, z_send, z_recv, f_send, f_recv, out_send, out_recv, pass_send, pass_recv, e_send, e_recv,
     ) = scratch
 
     row = lax.axis_index("aux")
@@ -122,6 +122,12 @@
             slab_recv.at[k, i], pair=to_pair(i),
         )
 
+    def inter_copy(i, source):
+        return remote(
+            inter_hbm.at[pl.ds(to_aux(i) * share, share)], inter.at[source], inter_send.at[i],
+            inter_recv.at[i], aux=to_aux(i),
+        )
+
     for k in range(CHUNKS):
         rows = slice(starts[k], starts[k + 1])
 
@@ -133,15 +139,9 @@
 
         loop(clusters - 1, send_slab)
         incoming[k][cluster] = slab[table[cluster], rows, :]
-
-    def inter_copy(i, source):
-        return remote(
-            inter_hbm.at[pl.ds(to_aux(i) * share, share)], inter.at[source], inter_send.at[i],
-            inter_recv.at[i], aux=to_aux(i),
-        )
-
-    for i in range(1, groups):
-        inter_copy(i, row).start()
+        if k == 0:
+            for i in range(1, groups):
+                inter_copy(i, row).start()
 
     def denominators(q):
         p = cluster * pair_count + row * share + q
@@ -180,20 +180,25 @@
         )
 
     def send_part(q):
-        for i in range(1, groups):
+        for i in range(groups):
+            project_head(HEAD - 1, to_aux(i) * share + q)
+        parts = []
+        for i in range(groups):
             p = to_aux(i) * share + q
-            project_head(HEAD - 1, p)
-            part_out[i - 1, q] = dot(left[p], right[p], (0, 0)).astype(BF16)
+            parts.append(dot(left[p], right[p], (0, 0)))
+        coulomb[q] = parts[0]
+        for i in range(1, groups):
+            part_out[i - 1, q] = parts[i].astype(BF16)
+        for i in range(1, groups):
             part_copy(i, q).start()
-        p = row * share + q
-        project_head(HEAD - 1, p)
-        coulomb[q] = dot(left[p], right[p], (0, 0))
 
     def send_tail(k, q):
-        for i in range(1, groups):
-            tail_out[k - HEAD][i - 1, q] = project(k, to_aux(i) * share + q)
+        parts = [project(k, to_aux(i) * share + q) for i in range(groups)]
+        tail_in[k - HEAD][0, q] = parts[0]
+        for i in range(1, groups):
+            tail_out[k - HEAD][i - 1, q] = parts[i]
+        for i in range(1, groups):
             tail_copy(k, i, q).start()
-        tail_in[k - HEAD][0, q] = project(k, row * share + q)
 
     for k in range(CHUNKS):
         loop(clusters - 1, lambda j, k=k: slab_copy(k, far_first(j), from_pair(far_first(j))).wait_recv())
@@ -257,6 +262,24 @@
 
     loop(share, start_amplitude)
 
+    if groups == 4:
+        near = (row + 1 - 2 * lax.rem(row, 2), lax.rem(row + 2, 4))
+    else:
+        near = tuple(to_aux(i) for i in range(1, groups))
+    senders = near if groups == 4 else tuple(from_aux(i) for i in range(1, groups))
+
+    def out_copy(n, q, source):
+        return remote(
+            half.at[q], out_hbm.at[source * share + q], out_send.at[n, q], out_recv.at[n, q],
+            aux=near[n],
+        )
+
+    def pass_copy(n, q, source):
+        piece_of = out_hbm.at[source * share + q, pl.ds(n * (width // 2), width // 2), :]
+        return remote(
+            piece_of, piece_of, pass_send.at[n, q], pass_recv.at[n, q], aux=near[1 - n]
+        )
+
     for t in range(ITERS):
         def quadratic(q):
             product = dot(half[q], coulomb_half[q], (1, 1)).astype(BF16)
@@ -304,30 +327,26 @@
 
         def update(q, t=t):
             p = cluster * pair_count + row * share + q
+            rotated = []
+            for r in range(ref_cols):
+                partner = fetched[refs[r, p] // pair_count].reshape(width, width)
+                overlap = inter[r // local_cols, q, r % local_cols]
+                rotated.append(dot(overlap, partner, (1, 0)).astype(BF16))
             coupled = jnp.zeros((width, width), F32)
             for r in range(ref_cols):
-                source = refs[r, p] // pair_count
                 overlap = inter[r // local_cols, q, r % local_cols]
-                partner = fetched[source].reshape(width, width)
-                rotated = dot(overlap, partner, (1, 0)).astype(BF16)
-                coupled = coupled + dot(rotated, overlap, (1, 1))
+                coupled = coupled + dot(rotated[r], overlap, (1, 1))
             value = amp[q] + damping * coupled * rden[q]
+            value = weight(q) * value
             if t < ITERS - 1:
-                value = weight(q) * value
                 amp[q] = value
                 set_half(t + 1, q, value)
             else:
                 half[q] = value.astype(BF16)
-                for i in range(1, groups):
-                    out_copy(i, q, row).start()
-                total = jnp.sum(coulomb[q] * value, axis=0, keepdims=True) * weight(q)
+                for n in range(len(near)):
+                    out_copy(n, q, row).start()
+                total = jnp.sum(coulomb[q] * value, axis=0, keepdims=True)
                 energy_row[q] = total
-
-        def out_copy(i, q, source):
-            return remote(
-                half.at[q], out_hbm.at[source * share + q], out_send.at[i, q], out_recv.at[i, q],
-                aux=to_aux(i),
-            )
 
         loop(share, update)
 
@@ -342,6 +361,15 @@
     for i in range(1, groups):
         e_copy(i, row).start()
     energy_out[pl.ds(row * share, share)] = energy_row[...]
+
+    for n in range(len(near)):
+
+        def passing(q, n=n):
+            out_copy(n, q, senders[n]).wait_recv()
+            if groups == 4:
+                pass_copy(n, q, near[n]).start()
+
+        loop(share, passing)
 
     for k in range(CHUNKS):
         loop(clusters - 1, lambda j, k=k: slab_copy(k, j + 1, cluster).wait_send())
@@ -356,11 +384,14 @@
             loop(share, lambda q, t=t, i=i: split_copy(t, i, q, row).wait_send())
             loop(clusters, lambda j, t=t, i=i: f_copy(t, i, j, from_pair(j), row).wait_send())
     for i in range(1, groups):
-        loop(share, lambda q, i=i: out_copy(i, q, row).wait_send())
-        loop(share, lambda q, i=i: out_copy(i, q, from_aux(i)).wait_recv())
         e_copy(i, row).wait_send()
         e_copy(i, from_aux(i)).wait_recv()
     out_own.wait()
+    for n in range(len(near)):
+        loop(share, lambda q, n=n: out_copy(n, q, row).wait_send())
+        if groups == 4:
+            loop(share, lambda q, n=n: pass_copy(n, q, near[n]).wait_send())
+            loop(share, lambda q, n=n: pass_copy(n, q, 3 - row).wait_recv())
 
 
 def on_device(
@@ -408,7 +439,8 @@
             dma(groups, share), dma(groups, share), dma(CHUNKS - HEAD, groups, share),
             dma(CHUNKS - HEAD, groups, share), dma(ITERS, groups, share), dma(ITERS, groups, share),
             dma(ITERS, clusters), dma(ITERS, clusters), dma(ITERS, groups, clusters),
-            dma(ITERS, groups, clusters), dma(groups, share), dma(groups, share), dma(groups),
+            dma(ITERS, groups, clusters), dma(groups, share), dma(groups, share), dma(groups, share),
+            dma(groups, share), dma(groups),
             dma(groups),
         ]
     )
@@ -432,7 +464,6 @@
         pair_orbitals.T, partners.T, live, occ_energy, orbital_slabs, pno_energy, pno_maps,
         intersections,
     )
-    result = jnp.where(live[:, None, None] > 0, result, jnp.zeros_like(result))
     return result, jnp.sum(energy, axis=(1, 2))
 
 

time: 183 us -> 176 us (0.962)
  Pallas kernels: 177 us -> 170 us
  local copies, waits for them, and re-layouts: 0.01 us -> 3.09 us
  other arithmetic: 4.5 us -> 1.43 us
    pallas_call x1, Pallas kernels: 177 us -> 170 us  [on_device(): pl.pallas_call(functools.partial(kernel, groups, clusters), out_shape=(ja...]
    select_n x1 -> x0, other arithmetic: 3.12 us -> none  [on_device(): result = jnp.where(live[:, None, None] > 0, result, jnp.zeros_like(result))]
    unnamed x2 -> x1, local copies, waits for them, and re-layouts: 0.01 us -> 3.09 us
where the time goes in v4:
time: 176 us; the launch traced here: 175 us
  Pallas kernels  170 us (97%)
  local copies, waits for them, and re-layouts  3.09 us (2%)
    pallas_call x1, Pallas kernels, on_device(): pl.pallas_call(functools.partial(kernel, groups, clusters), out_shape=(ja...  170 us

profile of v4, /device:TPU:0, one launch (start us, length us, event | category | flops | bytes accessed | tf_op | source)
XLA Modules:
  0.0 175.2 jit_solution(9876752979196719446)
XLA Ops:
  0.6 170.1 %local_pair_amplitudes.1 = (bf16[16,256,256]{2,1,0:T(8,128)(2,1)}, f32[16,1,256]{2,1,0:T(1,128)}) custom-call(s32[2,128]{1,0:T(2,128)} %bitcast.3, s32[8,128]{1,0:T(8,128)} %bitcast.2, s32[16]{0:T(128)} %live.1, f32[32]{0:T(128)} %occ.1, bf16[4,256,768]{2,1,0:T(8,128)(2,1)} %slab.1, f32[16,256]{1,0:T(8,128)} %energy.1, bf16[16,768,256]{2,1,0:T(8,128)(2,1)} %maps_hbm.1, ...), custom_call_target="tpu_custom_call" | custom-call | tf_op jit(solution)/shard_map/local_pair_amplitudes/pallas_call | solution.py:450
  170.7 1.4 reduce_sum.9
  172.1 3.1 %copy.11 = bf16[16,256,256]{2,1,0:T(8,128)(2,1)} copy(bf16[16,256,256]{2,1,0:T(8,128)(2,1)} %get-tuple-element.8) | data formatting | bytes 4194304

commit v5 on v4

--- a/solution.py
+++ b/solution.py
@@ -8,7 +8,7 @@
 from jax.sharding import PartitionSpec as P
 
 ITERS = 2
-PARTS = (6, 6, 4)
+PARTS = (5, 5, 4, 2)
 CHUNKS = len(PARTS)
 HEAD = 2
 damping = 0.7
@@ -240,11 +240,7 @@
         quarter[t][row * share + q] = split[t][row, q]
 
     def start_amplitude(q):
-        for i in range(1, groups):
-            part_copy(i, q).wait_recv()
         total = coulomb[q]
-        for i in range(1, groups):
-            total = total + part_in[i - 1, q].astype(F32)
         lefts, rights = [], []
         for k in range(HEAD, CHUNKS):
             count = starts[k + 1] - starts[k]
@@ -260,6 +256,15 @@
         amp[q] = value
         set_half(0, q, value)
 
+    def add_parts(q):
+        for i in range(1, groups):
+            part_copy(i, q).wait_recv()
+        total = coulomb[q]
+        for i in range(1, groups):
+            total = total + part_in[i - 1, q].astype(F32)
+        coulomb[q] = total
+
+    loop(share, add_parts)
     loop(share, start_amplitude)
 
     if groups == 4:
@@ -362,14 +367,13 @@
         e_copy(i, row).start()
     energy_out[pl.ds(row * share, share)] = energy_row[...]
 
-    for n in range(len(near)):
-
-        def passing(q, n=n):
+    def passing(q):
+        for n in range(len(near)):
             out_copy(n, q, senders[n]).wait_recv()
             if groups == 4:
                 pass_copy(n, q, near[n]).start()
 
-        loop(share, passing)
+    loop(share, passing)
 
     for k in range(CHUNKS):
         loop(clusters - 1, lambda j, k=k: slab_copy(k, j + 1, cluster).wait_send())

time: 176 us -> 178 us (1.011)
  Pallas kernels: 170 us -> 173 us
    pallas_call x1, Pallas kernels: 170 us -> 173 us  [on_device(): pl.pallas_call(functools.partial(kernel, groups, clusters), out_shape=(ja...]
where the time goes in v5:
time: 178 us
  Pallas kernels  173 us (97%)
  local copies, waits for them, and re-layouts  3.09 us (2%)
    pallas_call x1, Pallas kernels, on_device(): pl.pallas_call(functools.partial(kernel, groups, clusters), out_shape=(ja...  173 us

profile of v5, /device:TPU:0, one launch (start us, length us, event | category | flops | bytes accessed | tf_op | source)
XLA Modules:
  0.0 177.9 jit_solution(13235513639964025306)
XLA Ops:
  0.6 172.8 %local_pair_amplitudes.1 = (bf16[16,256,256]{2,1,0:T(8,128)(2,1)}, f32[16,1,256]{2,1,0:T(1,128)}) custom-call(s32[2,128]{1,0:T(2,128)} %bitcast.3, s32[8,128]{1,0:T(8,128)} %bitcast.2, s32[16]{0:T(128)} %live.1, f32[32]{0:T(128)} %occ.1, bf16[4,256,768]{2,1,0:T(8,128)(2,1)} %slab.1, f32[16,256]{1,0:T(8,128)} %energy.1, bf16[16,768,256]{2,1,0:T(8,128)(2,1)} %maps_hbm.1, ...), custom_call_target="tpu_custom_call" | custom-call | tf_op jit(solution)/shard_map/local_pair_amplitudes/pallas_call | solution.py:454
  173.4 1.4 reduce_sum.9
  174.8 3.1 %copy.11 = bf16[16,256,256]{2,1,0:T(8,128)(2,1)} copy(bf16[16,256,256]{2,1,0:T(8,128)(2,1)} %get-tuple-element.8) | data formatting | bytes 4194304

commit v6 on v5

--- a/solution.py
+++ b/solution.py
@@ -8,7 +8,7 @@
 from jax.sharding import PartitionSpec as P
 
 ITERS = 2
-PARTS = (5, 5, 4, 2)
+PARTS = (6, 6, 4)
 CHUNKS = len(PARTS)
 HEAD = 2
 damping = 0.7
@@ -78,6 +78,20 @@
     def from_aux(i):
         return lax.rem(row + groups - i, groups)
 
+    four = groups == 4
+    if four:
+        near = (row + 1 - 2 * lax.rem(row, 2), lax.rem(row + 2, 4))
+        senders = near
+    else:
+        near = tuple(to_aux(i) for i in range(1, groups))
+        senders = tuple(from_aux(i) for i in range(1, groups))
+    far = groups - 1 - row
+    hops = range(len(near))
+
+    def half_of(ref, n):
+        rows = ref.shape[0] // 2
+        return ref.at[pl.ds(n * rows, rows), :]
+
     def far_first(j):
         return lax.rem(clusters // 2 - 1 + j, clusters - 1) + 1
 
@@ -167,10 +181,16 @@
         left[p, starts[k]:starts[k + 1], :] = both[:count]
         right[p, starts[k]:starts[k + 1], :] = both[count:]
 
-    def part_copy(i, q):
-        return remote(
-            part_out.at[i - 1, q], part_in.at[i - 1, q], part_send.at[i, q], part_recv.at[i, q],
-            aux=to_aux(i),
+    def part_copy(n, q):
+        return remote(
+            part_out.at[n, q], part_in.at[n, q], part_send.at[n, q], part_recv.at[n, q],
+            aux=near[n],
+        )
+
+    def far_copy(n, q):
+        return remote(
+            half_of(part_out.at[2, q], n), half_of(part_in.at[2, q], n), part_send.at[2 + n, q],
+            part_recv.at[2 + n, q], aux=near[n],
         )
 
     def tail_copy(k, i, q):
@@ -179,18 +199,38 @@
             tail_send.at[k - HEAD, i, q], tail_recv.at[k - HEAD, i, q], aux=to_aux(i),
         )
 
+    def head_sum(p):
+        project_head(HEAD - 1, p)
+        return dot(left[p], right[p], (0, 0))
+
+    def send_far(q):
+        part_out[2, q] = head_sum(far * share + q).astype(BF16)
+        for n in hops:
+            far_copy(n, q).start()
+
+    def own_part(q):
+        coulomb[q] = head_sum(row * share + q)
+
     def send_part(q):
-        for i in range(groups):
-            project_head(HEAD - 1, to_aux(i) * share + q)
-        parts = []
-        for i in range(groups):
-            p = to_aux(i) * share + q
-            parts.append(dot(left[p], right[p], (0, 0)))
-        coulomb[q] = parts[0]
-        for i in range(1, groups):
-            part_out[i - 1, q] = parts[i].astype(BF16)
-        for i in range(1, groups):
-            part_copy(i, q).start()
+        sums = [head_sum(near[n] * share + q) for n in hops]
+        for n in hops:
+            total = sums[n]
+            if four:
+                far_copy(1 - n, q).wait_recv()
+                rows = width // 2
+                passing_by = part_in[2, q, (1 - n) * rows:(2 - n) * rows, :].astype(F32)
+                parts = [total[:rows], total[rows:]]
+                parts[1 - n] = parts[1 - n] + passing_by
+                total = jnp.concatenate(parts, axis=0)
+            part_out[n, q] = total.astype(BF16)
+        for n in hops:
+            part_copy(n, q).start()
+
+    def send_head():
+        if four:
+            loop(share, send_far)
+        loop(share, own_part)
+        loop(share, send_part)
 
     def send_tail(k, q):
         parts = [project(k, to_aux(i) * share + q) for i in range(groups)]
@@ -205,7 +245,7 @@
         if k < HEAD - 1:
             loop(pair_count, lambda p, k=k: project_head(k, p))
         elif k == HEAD - 1:
-            loop(share, send_part)
+            send_head()
         else:
             loop(share, lambda q, k=k: send_tail(k, q))
 
@@ -221,10 +261,17 @@
             pair=to_pair(i),
         )
 
-    def f_copy(t, i, j, member, source):
-        return remote(
-            zin[t].at[member], fetched.at[member, source], f_send.at[t, i, j],
-            f_recv.at[t, i, j], aux=to_aux(i),
+    def f_copy(t, n, j, source):
+        member = from_pair(j)
+        return remote(
+            zin[t].at[member], fetched.at[member, source], f_send.at[t, n, j], f_recv.at[t, n, j],
+            aux=near[n],
+        )
+
+    def f_pass(t, n, j, source):
+        piece_of = half_of(fetched.at[from_pair(j), source], n)
+        return remote(
+            piece_of, piece_of, f_send.at[t, 2 + n, j], f_recv.at[t, 2 + n, j], aux=near[1 - n]
         )
 
     def weight(q):
@@ -257,22 +304,15 @@
         set_half(0, q, value)
 
     def add_parts(q):
-        for i in range(1, groups):
-            part_copy(i, q).wait_recv()
         total = coulomb[q]
-        for i in range(1, groups):
-            total = total + part_in[i - 1, q].astype(F32)
+        for n in hops:
+            part_copy(n, q).wait_recv()
+            total = total + part_in[n, q].astype(F32)
         coulomb[q] = total
 
     loop(share, add_parts)
     loop(share, start_amplitude)
 
-    if groups == 4:
-        near = (row + 1 - 2 * lax.rem(row, 2), lax.rem(row + 2, 4))
-    else:
-        near = tuple(to_aux(i) for i in range(1, groups))
-    senders = near if groups == 4 else tuple(from_aux(i) for i in range(1, groups))
-
     def out_copy(n, q, source):
         return remote(
             half.at[q], out_hbm.at[source * share + q], out_send.at[n, q], out_recv.at[n, q],
@@ -280,7 +320,7 @@
         )
 
     def pass_copy(n, q, source):
-        piece_of = out_hbm.at[source * share + q, pl.ds(n * (width // 2), width // 2), :]
+        piece_of = half_of(out_hbm.at[source * share + q], n)
         return remote(
             piece_of, piece_of, pass_send.at[n, q], pass_recv.at[n, q], aux=near[1 - n]
         )
@@ -306,29 +346,35 @@
         mine = quarter[t][table[clusters + cluster]]
         zin[t][cluster] = mine
         fetched[cluster, row] = mine
-        for i in range(1, groups):
-            f_copy(t, i, 0, cluster, row).start()
+        for n in hops:
+            f_copy(t, n, 0, row).start()
         loop(share, quadratic)
+
+        def hand_on(j, t=t):
+            for n in hops:
+                f_copy(t, n, j, senders[n]).wait_recv()
+                if four:
+                    f_pass(t, n, j, near[n]).start()
 
         def forward(j, t=t):
             j = j + 1
             member = from_pair(j)
             z_copy(t, j, member).wait_recv()
-            for i in range(1, groups):
-                f_copy(t, i, j, member, row).start()
+            for n in hops:
+                f_copy(t, n, j, row).start()
             fetched[member, row] = zin[t][member]
+            hand_on(j - 1)
 
         loop(clusters - 1, forward)
+        hand_on(clusters - 1)
         if t == 0:
             inter_own.wait()
             for i in range(1, groups):
                 inter_copy(i, from_aux(i)).wait_recv()
-
-        def arrive(j, t=t):
-            for i in range(1, groups):
-                f_copy(t, i, j, from_pair(j), from_aux(i)).wait_recv()
-
-        loop(clusters, arrive)
+        if four:
+            for n in hops:
+                loop(clusters, lambda j, t=t, n=n: f_pass(t, n, j, far).wait_recv())
+                loop(clusters, lambda j, t=t, n=n: f_pass(t, n, j, near[n]).wait_send())
 
         def update(q, t=t):
             p = cluster * pair_count + row * share + q
@@ -348,7 +394,7 @@
                 set_half(t + 1, q, value)
             else:
                 half[q] = value.astype(BF16)
-                for n in range(len(near)):
+                for n in hops:
                     out_copy(n, q, row).start()
                 total = jnp.sum(coulomb[q] * value, axis=0, keepdims=True)
                 energy_row[q] = total
@@ -368,9 +414,9 @@
     energy_out[pl.ds(row * share, share)] = energy_row[...]
 
     def passing(q):
-        for n in range(len(near)):
+        for n in hops:
             out_copy(n, q, senders[n]).wait_recv()
-            if groups == 4:
+            if four:
                 pass_copy(n, q, near[n]).start()
 
     loop(share, passing)
@@ -379,21 +425,24 @@
         loop(clusters - 1, lambda j, k=k: slab_copy(k, j + 1, cluster).wait_send())
     for i in range(1, groups):
         inter_copy(i, row).wait_send()
-        loop(share, lambda q, i=i: part_copy(i, q).wait_send())
         for k in range(HEAD, CHUNKS):
             loop(share, lambda q, i=i, k=k: tail_copy(k, i, q).wait_send())
     for t in range(ITERS):
         loop(clusters - 1, lambda j, t=t: z_copy(t, j + 1, cluster).wait_send())
         for i in range(1, groups):
             loop(share, lambda q, t=t, i=i: split_copy(t, i, q, row).wait_send())
-            loop(clusters, lambda j, t=t, i=i: f_copy(t, i, j, from_pair(j), row).wait_send())
+        for n in hops:
+            loop(clusters, lambda j, t=t, n=n: f_copy(t, n, j, row).wait_send())
     for i in range(1, groups):
         e_copy(i, row).wait_send()
         e_copy(i, from_aux(i)).wait_recv()
     out_own.wait()
-    for n in range(len(near)):
+    for n in hops:
+        loop(share, lambda q, n=n: part_copy(n, q).wait_send())
+        if four:
+            loop(share, lambda q, n=n: far_copy(n, q).wait_send())
         loop(share, lambda q, n=n: out_copy(n, q, row).wait_send())
-        if groups == 4:
+        if four:
             loop(share, lambda q, n=n: pass_copy(n, q, near[n]).wait_send())
             loop(share, lambda q, n=n: pass_copy(n, q, 3 - row).wait_recv())
 

time: 178 us -> 174 us (0.978)
  Pallas kernels: 173 us -> 169 us
    pallas_call x1, Pallas kernels: 173 us -> 169 us  [on_device(): pl.pallas_call(functools.partial(kernel, groups, clusters), out_shape=(ja...]
where the time goes in v6:
time: 174 us
  Pallas kernels  169 us (97%)
  local copies, waits for them, and re-layouts  3.09 us (2%)
    pallas_call x1, Pallas kernels, on_device(): pl.pallas_call(functools.partial(kernel, groups, clusters), out_shape=(ja...  169 us

profile of v6, /device:TPU:0, one launch (start us, length us, event | category | flops | bytes accessed | tf_op | source)
XLA Modules:
  0.0 173.8 jit_solution(2166858388581024541)
XLA Ops:
  0.6 168.7 %local_pair_amplitudes.1 = (bf16[16,256,256]{2,1,0:T(8,128)(2,1)}, f32[16,1,256]{2,1,0:T(1,128)}) custom-call(s32[2,128]{1,0:T(2,128)} %bitcast.3, s32[8,128]{1,0:T(8,128)} %bitcast.2, s32[16]{0:T(128)} %live.1, f32[32]{0:T(128)} %occ.1, bf16[4,256,768]{2,1,0:T(8,128)(2,1)} %slab.1, f32[16,256]{1,0:T(8,128)} %energy.1, bf16[16,768,256]{2,1,0:T(8,128)(2,1)} %maps_hbm.1, ...), custom_call_target="tpu_custom_call" | custom-call | tf_op jit(solution)/shard_map/local_pair_amplitudes/pallas_call | solution.py:503
  169.3 1.4 reduce_sum.9
  170.8 3.1 %copy.11 = bf16[16,256,256]{2,1,0:T(8,128)(2,1)} copy(bf16[16,256,256]{2,1,0:T(8,128)(2,1)} %get-tuple-element.8) | data formatting | bytes 4194304

commit v7 on v6

--- a/solution.py
+++ b/solution.py
@@ -136,12 +136,17 @@
             slab_recv.at[k, i], pair=to_pair(i),
         )
 
-    def inter_copy(i, source):
-        return remote(
-            inter_hbm.at[pl.ds(to_aux(i) * share, share)], inter.at[source], inter_send.at[i],
-            inter_recv.at[i], aux=to_aux(i),
-        )
-
+    def inter_copy(i, q, source):
+        return remote(
+            inter_hbm.at[to_aux(i) * share + q], inter.at[source, q], inter_send.at[i, q],
+            inter_recv.at[i, q], aux=to_aux(i),
+        )
+
+    def send_inter(q):
+        for i in range(1, groups):
+            inter_copy(i, q, row).start()
+
+    mixed = min(share, clusters - 1)
     for k in range(CHUNKS):
         rows = slice(starts[k], starts[k + 1])
 
@@ -151,11 +156,17 @@
             staged[k][to] = slab[table[to], rows, :]
             slab_copy(k, i, cluster).start()
 
-        loop(clusters - 1, send_slab)
+        def send_both(j, send_slab=send_slab):
+            send_slab(j)
+            send_inter(j)
+
+        if k == 0:
+            loop(mixed, send_both)
+            loop(clusters - 1 - mixed, lambda j, send_slab=send_slab: send_slab(j + mixed))
+            loop(share - mixed, lambda q: send_inter(q + mixed))
+        else:
+            loop(clusters - 1, send_slab)
         incoming[k][cluster] = slab[table[cluster], rows, :]
-        if k == 0:
-            for i in range(1, groups):
-                inter_copy(i, row).start()
 
     def denominators(q):
         p = cluster * pair_count + row * share + q
@@ -370,7 +381,7 @@
         if t == 0:
             inter_own.wait()
             for i in range(1, groups):
-                inter_copy(i, from_aux(i)).wait_recv()
+                loop(share, lambda q, i=i: inter_copy(i, q, from_aux(i)).wait_recv())
         if four:
             for n in hops:
                 loop(clusters, lambda j, t=t, n=n: f_pass(t, n, j, far).wait_recv())
@@ -424,7 +435,7 @@
     for k in range(CHUNKS):
         loop(clusters - 1, lambda j, k=k: slab_copy(k, j + 1, cluster).wait_send())
     for i in range(1, groups):
-        inter_copy(i, row).wait_send()
+        loop(share, lambda q, i=i: inter_copy(i, q, row).wait_send())
         for k in range(HEAD, CHUNKS):
             loop(share, lambda q, i=i, k=k: tail_copy(k, i, q).wait_send())
     for t in range(ITERS):
@@ -488,7 +499,7 @@
         + [vm((clusters, piece, width), BF16)] * (2 * ITERS)
         + [vm((clusters, groups, piece, width), BF16)]
         + [
-            dma(3), dma(groups), dma(groups), dma(CHUNKS, clusters), dma(CHUNKS, clusters),
+            dma(3), dma(groups, share), dma(groups, share), dma(CHUNKS, clusters), dma(CHUNKS, clusters),
             dma(groups, share), dma(groups, share), dma(CHUNKS - HEAD, groups, share),
             dma(CHUNKS - HEAD, groups, share), dma(ITERS, groups, share), dma(ITERS, groups, share),
             dma(ITERS, clusters), dma(ITERS, clusters), dma(ITERS, groups, clusters),

time: 174 us -> 174 us (level)
  no operation moved by 1% of the time
where the time goes in v7:
time: 174 us
  Pallas kernels  169 us (97%)
  local copies, waits for them, and re-layouts  3.09 us (2%)
    pallas_call x1, Pallas kernels, on_device(): pl.pallas_call(functools.partial(kernel, groups, clusters), out_shape=(ja...  169 us

profile of v7, /device:TPU:0, one launch (start us, length us, event | category | flops | bytes accessed | tf_op | source)
XLA Modules:
  0.0 174.1 jit_solution(15452598040787967096)
XLA Ops:
  0.6 168.9 %local_pair_amplitudes.1 = (bf16[16,256,256]{2,1,0:T(8,128)(2,1)}, f32[16,1,256]{2,1,0:T(1,128)}) custom-call(s32[2,128]{1,0:T(2,128)} %bitcast.3, s32[8,128]{1,0:T(8,128)} %bitcast.2, s32[16]{0:T(128)} %live.1, f32[32]{0:T(128)} %occ.1, bf16[4,256,768]{2,1,0:T(8,128)(2,1)} %slab.1, f32[16,256]{1,0:T(8,128)} %energy.1, bf16[16,768,256]{2,1,0:T(8,128)(2,1)} %maps_hbm.1, ...), custom_call_target="tpu_custom_call" | custom-call | tf_op jit(solution)/shard_map/local_pair_amplitudes/pallas_call | solution.py:514
  169.5 1.4 reduce_sum.9
  171.0 3.1 %copy.11 = bf16[16,256,256]{2,1,0:T(8,128)(2,1)} copy(bf16[16,256,256]{2,1,0:T(8,128)(2,1)} %get-tuple-element.8) | data formatting | bytes 4194304
